TPU v7x, 128 devices: a whole 4x4x4 slice. The times are simulated.
128 devices in a mesh: space: 32 (over x, y, core), chan: 4 (over z).
Axes of the slice: x: 4, y: 4, z: 4, core: 2. Of those that a mesh axis runs over, the one named last changes fastest.
Arguments:
- grid_state: bfloat16 [262144, 512], P('space', 'chan'), may hold values from -6 to 6
- cotangent: bfloat16 [262144, 512], P('space', 'chan'), may hold values from -6 to 6
- encoder_weight: bfloat16 [512, 512], P(None, 'chan'), may hold values from -0.25 to 0.25
- processor_weight: bfloat16 [512, 512], P(None, 'chan'), may hold values from -0.25 to 0.25
- decoder_weight: bfloat16 [512, 512], P(None, 'chan'), may hold values from -0.25 to 0.25
- g2m_send: int32 [1024, 256], P('space'), may hold values from 0 to 8191
- g2m_edges: int32 [10240, 40], P('space'), may hold values from 0 to 8191, as said below
- m2g_send: int32 [1024, 40], P('space'), may hold values from 0 to 319
- m2g_edges: int32 [262144, 3], P('space'), may hold values from 0 to 1279
- m2m_edges: int32 [10240, 8], P('space'), may hold values from 0 to 10239, as said below
Outputs:
- prediction: bfloat16 [262144, 512], P('space', 'chan')
- grad_encoder: float32 [512, 512], P(None, 'chan')
- grad_processor: float32 [512, 512], P(None, 'chan')
- grad_decoder: float32 [512, 512], P(None, 'chan')
Inputs may be any that keep to these rules, and one draw needn't show every extreme that they name: `g2m_send`: row s times the number of space devices plus p lists, slot by slot, the grid row local to device s that fills that slot for mesh owner p; a row may fill several slots. `g2m_edges`: each value is a slot of the rows received by the mesh node's own device; every such slot is named by some mesh node of that device. `m2g_send`: row s times the number of space devices plus p lists, slot by slot, the mesh row local to device s that fills that slot for grid owner p. `m2g_edges`: each value is a slot of the rows received by the grid node's own device. `m2m_edges`: each neighbour of mesh node m lies within 160 rows of m, counted cyclically over all 10240 rows.
All inputs are finite; a program needn't handle non-finite values.
Results may differ from a plain program's by a relative error of at most 0.0065.
Values may be sent and summed in bfloat16 or wider, within the bound.
A program may use at most 128 MiB of HBM per device.

v0:
```python
import jax
import jax.numpy as jnp
from jax import lax
from jax.sharding import PartitionSpec as P

FAN_G2M = 40
FAN_M2M = 8
FAN_M2G = 3
REACH = 160


def extended_2(cells, sides, width):
    for axis, dim in sides:
        count = lax.axis_size(axis)
        head = lax.slice_in_dim(cells, 0, width, axis=dim)
        tail = lax.slice_in_dim(cells, cells.shape[dim] - width, cells.shape[dim], axis=dim)
        cells = jnp.concatenate(
            [
                lax.ppermute(tail, axis, [(i, (i + 1) % count) for i in range(count)]),
                cells,
                lax.ppermute(head, axis, [((i + 1) % count, i) for i in range(count)]),
            ],
            axis=dim,
        )
    return cells


def from_behind(x, axis, by):
    devices = lax.axis_size(axis)
    return lax.ppermute(x, axis, [(i, (i + by) % devices) for i in range(devices)])


def silu_slope(values):
    sigmoid = jax.nn.sigmoid(values)
    return sigmoid * (1.0 + values * (1.0 - sigmoid))


def fold_weight(weight, feature_piece):
    return jnp.dot(feature_piece, weight, preferred_element_type=jnp.float32)


def edge_counts(indices, width):
    row_ids = lax.broadcasted_iota(jnp.int32, indices.shape, 0)
    counts = jnp.zeros((indices.shape[0], width), jnp.bfloat16)
    return counts.at[row_ids, indices].add(jnp.ones(indices.shape, jnp.bfloat16))


def gather_sum(table, indices):
    summed = jnp.zeros((indices.shape[0], table.shape[1]), jnp.float32)
    for column in range(indices.shape[1]):
        summed = summed + table[indices[:, column]].astype(jnp.float32)
    return summed


def spread_sum(values, indices, segment_count):
    summed = jnp.zeros((segment_count, values.shape[1]), jnp.float32)
    for column in range(indices.shape[1]):
        summed = summed.at[indices[:, column]].add(values)
    return summed


def exact_dot(left, right):
    return jnp.dot(
        left,
        right.astype(jnp.float32),
        precision=lax.Precision.HIGHEST,
        preferred_element_type=jnp.float32,
    )


def lead_dot(left, right):
    return lax.dot_general(
        left.astype(jnp.float32),
        right,
        (((0,), (0,)), ((), ())),
        precision=lax.Precision.HIGHEST,
        preferred_element_type=jnp.float32,
    )


def local(
    grid_state,
    cotangent,
    encoder_weight,
    processor_weight,
    decoder_weight,
    g2m_send,
    g2m_edges,
    m2g_send,
    m2g_edges,
    m2m_edges,
):
    peer_count = lax.axis_size("space")
    own_index = lax.axis_index("space")
    mesh_rows = g2m_edges.shape[0]
    column_count = encoder_weight.shape[1]
    grid_slots = peer_count * g2m_send.shape[1]
    mesh_slots = peer_count * m2g_send.shape[1]
    g2m_scale = FAN_G2M ** (-0.5)
    m2m_scale = FAN_M2M ** (-0.5)
    m2g_scale = FAN_M2G ** (-0.5)
    send_flat = g2m_send.reshape(-1)
    received = lax.all_to_all(
        grid_state[g2m_send], "space", split_axis=0, concat_axis=0, tiled=True
    )
    state_slots = received.reshape(grid_slots, column_count)
    encoded_slots = fold_weight(
        encoder_weight, lax.all_gather(state_slots, "chan", axis=1, tiled=True)
    ).astype(jnp.bfloat16)
    g2m_matrix = edge_counts(g2m_edges, grid_slots)
    gathered_sum = (
        jnp.dot(g2m_matrix, encoded_slots, preferred_element_type=jnp.float32) * g2m_scale
    )
    mesh_first = jax.nn.silu(gathered_sum).astype(jnp.bfloat16)
    projected = fold_weight(
        processor_weight, lax.all_gather(mesh_first, "chan", axis=1, tiled=True)
    ).astype(jnp.bfloat16)
    extended = extended_2(projected, (("space", 0),), REACH)
    node_rows = lax.broadcasted_iota(jnp.int32, m2m_edges.shape, 0)
    mesh_total = peer_count * mesh_rows
    rim_index = (m2m_edges - own_index * mesh_rows - node_rows + REACH) % mesh_total + node_rows
    rim_matrix = edge_counts(rim_index, mesh_rows + 2 * REACH)
    neighbour_sum = jnp.dot(rim_matrix, extended, preferred_element_type=jnp.float32) * m2m_scale
    mesh_second = (mesh_first.astype(jnp.float32) + jax.nn.silu(neighbour_sum)).astype(jnp.bfloat16)
    decoded = fold_weight(
        decoder_weight, lax.all_gather(mesh_second, "chan", axis=1, tiled=True)
    ).astype(jnp.bfloat16)
    mesh_send_flat = m2g_send.reshape(-1)
    outgoing = decoded[mesh_send_flat]
    returned = lax.all_to_all(
        outgoing.reshape(peer_count, -1, column_count),
        "space",
        split_axis=0,
        concat_axis=0,
        tiled=True,
    )
    decoded_slots = returned.reshape(mesh_slots, column_count)
    prediction = (
        grid_state.astype(jnp.float32) + gather_sum(decoded_slots, m2g_edges) * m2g_scale
    ).astype(jnp.bfloat16)
    mesh_slot_grad = spread_sum(cotangent.astype(jnp.float32) * m2g_scale, m2g_edges, mesh_slots)
    sent_back = lax.all_to_all(
        mesh_slot_grad.reshape(peer_count, -1, column_count),
        "space",
        split_axis=0,
        concat_axis=0,
        tiled=True,
    )
    decoded_grad = (
        jnp.zeros((mesh_rows, column_count), jnp.float32)
        .at[mesh_send_flat]
        .add(sent_back.reshape(mesh_slots, column_count))
    )
    second_full = lax.all_gather(mesh_second, "chan", axis=1, tiled=True)
    grad_decoder = lead_dot(second_full, decoded_grad)
    second_grad = lax.psum_scatter(
        exact_dot(decoded_grad, decoder_weight.T), "chan", scatter_dimension=1, tiled=True
    )
    pre_grad = second_grad * silu_slope(neighbour_sum) * m2m_scale
    rim_grad = lead_dot(rim_matrix, pre_grad)
    from_upper = from_behind(rim_grad[:REACH], "space", -1)
    from_lower = from_behind(rim_grad[REACH + mesh_rows :], "space", 1)
    inside_rows = rim_grad[REACH : REACH + mesh_rows]
    projected_grad = inside_rows.at[:REACH].add(from_lower).at[mesh_rows - REACH :].add(from_upper)
    first_full = lax.all_gather(mesh_first, "chan", axis=1, tiled=True)
    grad_processor = lead_dot(first_full, projected_grad)
    first_grad = second_grad + lax.psum_scatter(
        exact_dot(projected_grad, processor_weight.T), "chan", scatter_dimension=1, tiled=True
    )
    sum_grad = first_grad * silu_slope(gathered_sum) * g2m_scale
    slot_grad = lead_dot(g2m_matrix, sum_grad)
    grid_back = lax.all_to_all(
        slot_grad.reshape(peer_count, -1, column_count),
        "space",
        split_axis=0,
        concat_axis=0,
        tiled=True,
    )
    grid_full = lax.all_gather(grid_state, "chan", axis=1, tiled=True)
    sent_rows = grid_full[send_flat]
    grad_encoder = lead_dot(sent_rows, grid_back.reshape(grid_slots, column_count))
    grad_encoder, grad_processor, grad_decoder = lax.psum(
        (grad_encoder, grad_processor, grad_decoder), "space"
    )
    return (prediction, grad_encoder, grad_processor, grad_decoder)


def solution(mesh):
    placed = (
        P("space", "chan"),
        P("space", "chan"),
        P(None, "chan"),
        P(None, "chan"),
        P(None, "chan"),
        P("space", None),
        P("space", None),
        P("space", None),
        P("space", None),
        P("space", None),
    )
    return jax.shard_map(
        local,
        mesh=mesh,
        in_specs=placed,
        out_specs=(P("space", "chan"), P(None, "chan"), P(None, "chan"), P(None, "chan")),
        check_vma=False,
    )
```

profile of v0, /device:TPU:1, one launch (start us, length us, event | category | flops | bytes accessed | tf_op | source)
XLA Modules:
  0.0 749.4 jit_solution(2339426088904881107)
XLA Ops:
  7.2 0.8 fusion.40
  8.1 30.1 %gather_fusion = bf16[8192,128]{1,0:T(8,128)(2,1)} fusion(bf16[8192,128]{1,0:T(8,128)(2,1)} %param.14, s32[8192]{0:T(1024)S(1)} %broadcast_clamp_fusion.4), kind=kCustom, calls=%fused_computation | custom fusion | bytes 4227072 | tf_op jit(solution)/shard_map/gather | solution.py:104
  38.2 37.0 %all_to_all.20 = bf16[32,256,128]{2,1,0:T(8,128)(2,1)} all-to-all(bf16[32,256,128]{2,1,0:T(8,128)(2,1)} %bitcast.47), channel_id=1, replica_groups=mesh['space'=32,'chan'=4] {'space'}, dimensions={0} | all-to-all | bytes 4194304 | tf_op jit(solution)/shard_map/all_to_all | solution.py:103
  75.4 45.0 %scatter_custom_fusion = f32[1280,128]{1,0:T(8,128)} fusion(s32[8192]{0:T(1024)S(1)} %bitcast.58, bf16[8192,128]{1,0:T(8,128)(2,1)S(1)} %copy-done.3, f32[]{:T(128)} %constant.114.clone.1, f32[]{:T(128)} %constant.115.clone.1), kind=kCustom, calls=%fused_computation.16 | custom fusion | flops 3145728 | bytes 2752520 | tf_op jit(solution)/shard_map/scatter-add | solution.py:58
  120.4 41.7 %scatter_custom_fusion.1 = f32[1280,128]{1,0:T(8,128)} fusion(f32[1280,128]{1,0:T(8,128)} %scatter_custom_fusion, s32[8192]{0:T(1024)S(1)} %bitcast.56, bf16[8192,128]{1,0:T(8,128)(2,1)S(1)} %copy-done.3, f32[]{:T(128)} %constant.114.clone.1), kind=kCustom, calls=%fused_computation.15 | custom fusion | flops 3145728 | bytes 2753024 | tf_op jit(solution)/shard_map/scatter-add | solution.py:58
  162.1 41.7 %scatter_custom_fusion.2 = f32[1280,128]{1,0:T(8,128)} fusion(f32[1280,128]{1,0:T(8,128)} %scatter_custom_fusion.1, s32[8192]{0:T(1024)S(1)} %bitcast.54, bf16[8192,128]{1,0:T(8,128)(2,1)S(1)} %copy-done.3, f32[]{:T(128)} %constant.114.clone.1), kind=kCustom, calls=%fused_computation.14 | custom fusion | flops 3145728 | bytes 2753024 | tf_op jit(solution)/shard_map/scatter-add | solution.py:58
  203.8 4.0 all-to-all-start.2
  207.7 0.2 reduce-scatter.3.cloned.1.call-start
  208.3 0.1 reshape.261
  208.5 91.4 %scatter_custom_fusion.4 = bf16[2621440]{0:T(1024)(128)(2,1)} fusion(s32[12800]{0:T(1024)S(1)} %reshape.261, bf16[12800]{0:T(1024)(128)(2,1)S(1)} %broadcast.161, bf16[]{:T(256)} %constant.100.clone.1), kind=kCustom, calls=%fused_computation.18 | custom fusion | flops 12800 | bytes 5242882
  300.0 8.9 %reshape.176 = bf16[320,8192]{1,0:T(8,128)(2,1)} reshape(bf16[2621440]{0:T(1024)(128)(2,1)} %scatter_custom_fusion.4) | data formatting | bytes 10485760 | tf_op jit(solution)/shard_map/scatter-add | solution.py:45
  309.2 9.0 %scatter_custom_fusion.3 = f32[320,128]{1,0:T(8,128)S(1)} fusion(s32[1280]{0:T(1024)S(1)} %fusion.43, f32[1280,128]{1,0:T(8,128)S(1)} %bitcast.49, f32[]{:T(128)} %constant.115.clone.1), kind=kCustom, calls=%fused_computation.67 | custom fusion | flops 163840 | bytes 163844 | tf_op jit(solution)/shard_map/scatter-add | solution.py:152
  318.2 1.3 fusion.51
  319.5 0.4 reduce-scatter.5.cloned.1.call-start
  320.0 9.4 %multiply_convert_fusion = (bf16[320,128]{1,0:T(8,128)(2,1)S(1)}, f32[320,128]{1,0:T(8,128)S(1)}) fusion(bf16[320,8192]{1,0:T(8,128)(2,1)} %reshape.176, bf16[8192,512]{1,0:T(8,128)(2,1)} %all-gather.3.cloned.1.call-done, bf16[512,128]{1,0:T(8,128)(2,1)S(1)} %copy-done.15), kind=kOutput, calls=%fused_computation.57 | convolution fusion | flops 1746124800 | bytes 14008320 | tf_op jit(solution)/shard_map/dot_general | solution.py:112
  329.4 14.3 %all_gather.15 = bf16[320,512]{1,0:T(8,128)(2,1)S(1)} all-gather(bf16[320,128]{1,0:T(8,128)(2,1)S(1)} %get-tuple-element.38), channel_id=1, replica_groups=mesh['space'=32,'chan'=4] {'chan'}, dimensions={1}, use_global_device_ids=true | all-gather | bytes 409600 | tf_op jit(solution)/shard_map/all_gather | solution.py:116
  343.7 0.2 convolution_convert_fusion.2
  344.0 3.9 collective-permute-start
  348.0 0.1 reshape.267
  348.2 18.3 %scatter_custom_fusion.5 = bf16[204800]{0:T(1024)(128)(2,1)S(1)} fusion(s32[2560]{0:T(1024)S(1)} %reshape.267, bf16[2560]{0:T(1024)(128)(2,1)S(1)} %broadcast.163, bf16[]{:T(256)} %constant.100.clone.1), kind=kCustom, calls=%fused_computation.28 | custom fusion | flops 2560 | bytes 409602
  366.4 0.3 reshape.180
  366.8 0.3 add_convert_fusion.1
  367.1 1.6 fusion.24
  368.8 1.8 collective-permute-start.2
  370.6 1.9 collective-permute-start.3
  372.5 0.7 collective-permute-done.2
  373.2 1.4 collective-permute-done.3
  374.6 1.3 fusion.52
  375.9 0.5 all-gather.5.cloned.1.call-update
  376.5 9.2 %all_gather.16 = bf16[320,512]{1,0:T(8,128)(2,1)S(1)} all-gather(bf16[320,128]{1,0:T(8,128)(2,1)S(1)} %get-tuple-element.40), channel_id=1, replica_groups=mesh['space'=32,'chan'=4] {'chan'}, dimensions={1}, use_global_device_ids=true | all-gather | bytes 409600 | tf_op jit(solution)/shard_map/all_gather | solution.py:126
  385.7 0.2 convolution_convert_fusion.1
  385.9 3.5 gather_fusion.1
  389.4 12.3 %all-to-all-start.1 = ((bf16[32,40,128]{2,1,0:T(8,128)(2,1)}), bf16[32,40,128]{2,1,0:T(8,128)(2,1)S(1)}, u32[]{:S(2)}, u32[]{:S(2)}) async-start(bf16[32,40,128]{2,1,0:T(8,128)(2,1)} %bitcast.4), calls=%async_computation.1 | async-start | bytes 655360 | tf_op jit(solution)/shard_map/all_to_all | solution.py:130
  401.8 10.1 %fusion.16 = f32[8192,128]{1,0:T(8,128)} fusion(bf16[320,8192]{1,0:T(8,128)(2,1)} %reshape.176, f32[320,128]{1,0:T(8,128)S(1)} %get-tuple-element.39, f32[320,128]{1,0:T(8,128)S(1)} %copy-done.5, f32[320,128]{1,0:T(8,128)} %reduce-scatter.5.cloned.1.call-done), kind=kOutput, calls=%fused_computation.40 | convolution fusion | flops 4026941440 | bytes 9928704 | tf_op jit(solution)/shard_map/dot_general | solution.py:72
  411.9 8.2 %all-to-all-start.3 = ((f32[32,256,128]{2,1,0:T(8,128)}), f32[32,256,128]{2,1,0:T(8,128)}, u32[]{:S(2)}, u32[]{:S(2)}) async-start(f32[32,256,128]{2,1,0:T(8,128)} %bitcast.46), calls=%async_computation.5 | async-start | bytes 8388608 | tf_op jit(solution)/shard_map/all_to_all | solution.py:172
  420.4 69.9 %all-gather.5.cloned.1.call-done = bf16[8192,512]{1,0:T(8,128)(2,1)} async-done(((bf16[8192,128]{1,0:T(8,128)(2,1)}), bf16[8192,512]{1,0:T(8,128)(2,1)}) %all-gather.5.cloned.1.call-update) | async-done | bytes 8388624 | tf_op jit(solution)/shard_map/all_gather | solution.py:179
  490.2 38.4 %gather_fusion.5 = bf16[8192,512]{1,0:T(8,128)(2,1)} fusion(bf16[8192,512]{1,0:T(8,128)(2,1)} %all-gather.5.cloned.1.call-done, s32[8192]{0:T(1024)S(1)} %broadcast_clamp_fusion.3), kind=kCustom, calls=%fused_computation.5 | custom fusion | bytes 16809984 | tf_op jit(solution)/shard_map/gather | solution.py:180
  528.6 1.3 fusion.55
  529.9 1.3 fusion.54
  531.2 29.4 %gather_fusion.2 = bf16[8192,128]{1,0:T(8,128)(2,1)} fusion(bf16[1280,128]{1,0:T(8,128)(2,1)S(1)} %bitcast.43, s32[8192]{0:T(1024)S(1)} %broadcast_clamp_fusion.2), kind=kCustom, calls=%fused_computation.2 | custom fusion | bytes 4227072 | tf_op jit(solution)/shard_map/gather | solution.py:51
  560.6 29.4 %gather_fusion.3 = bf16[8192,128]{1,0:T(8,128)(2,1)} fusion(bf16[1280,128]{1,0:T(8,128)(2,1)S(1)} %bitcast.44, s32[8192]{0:T(1024)S(1)} %broadcast_clamp_fusion.1), kind=kCustom, calls=%fused_computation.3 | custom fusion | bytes 4227072 | tf_op jit(solution)/shard_map/gather | solution.py:51
  590.0 29.5 %gather_fusion.4 = bf16[8192,128]{1,0:T(8,128)(2,1)} fusion(bf16[1280,128]{1,0:T(8,128)(2,1)S(1)} %bitcast.45, s32[8192]{0:T(1024)S(1)} %broadcast_clamp_fusion), kind=kCustom, calls=%fused_computation.4 | custom fusion | bytes 4227072 | tf_op jit(solution)/shard_map/gather | solution.py:51
  619.5 13.0 %fusion.53 = f32[512,128]{1,0:T(8,128)} fusion(bf16[8192,512]{1,0:T(8,128)(2,1)} %gather_fusion.5, f32[8192,128]{1,0:T(8,128)} %bitcast.13), kind=kOutput, calls=%fused_computation.102 | convolution fusion | flops 6442450944 | bytes 12845056 | tf_op jit(solution)/shard_map/dot_general | solution.py:72
  632.5 5.4 add_convert_fusion
  637.9 99.7 %all-reduce.3.cloned.1.call-done = (f32[512,128]{1,0:T(8,128)}, f32[512,128]{1,0:T(8,128)}, f32[512,128]{1,0:T(8,128)}) async-done(((f32[512,128]{1,0:T(8,128)}, f32[512,128]{1,0:T(8,128)}, f32[512,128]{1,0:T(8,128)}), (f32[512,128]{1,0:T(8,128)}, f32[512,128]{1,0:T(8,128)}, f32[512,128]{1,0:T(8,128)})) %all-reduce.3.cloned.1.call-update) | async-done | bytes 786448 | tf_op jit(solution)/shard_map/psum | solution.py:182
  737.7 1.7 copy.25
  739.4 1.7 copy.26
  741.0 1.7 copy.27
  (79 shorter events, 1.4 us)
Async XLA Ops:
  7.2 336.6 %copy-start = (bf16[512,128]{1,0:T(8,128)(2,1)S(1)}, bf16[512,128]{1,0:T(8,128)(2,1)}, u32[]{:S(2)}) copy-start(bf16[512,128]{1,0:T(8,128)(2,1)} %param.17) | copy-start | bytes 393220
  7.2 312.8 %all-gather.3.cloned.1.call-start = ((), (), s32[]{:S(2)}) async-start(), calls=%async_computation.6 | async-start | bytes 10485760 | tf_op jit(solution)/shard_map/all_gather | solution.py:108
  38.2 37.0 %copy-start.7 = (s32[8192,3]{0,1:T(4,128)S(1)}, s32[8192,3]{0,1:T(4,128)}, u32[]{:S(2)}) copy-start(s32[8192,3]{0,1:T(4,128)} %param.22) | copy-start | bytes 294916
  38.2 37.1 %copy-start.3 = (bf16[8192,128]{1,0:T(8,128)(2,1)S(1)}, bf16[8192,128]{1,0:T(8,128)(2,1)}, u32[]{:S(2)}) copy-start(bf16[8192,128]{1,0:T(8,128)(2,1)} %param.15) | copy-start | bytes 6291460
  75.3 132.6 %copy-start.8 = (s32[320,40]{0,1:T(8,128)S(1)}, s32[320,40]{0,1:T(8,128)}, u32[]{:S(2)}) copy-start(s32[320,40]{0,1:T(8,128)} %param.20) | copy-start | bytes 153604
  75.3 132.7 %copy-start.14 = (s32[2]{0:T(128)S(1)}, s32[2]{0:T(128)}, u32[]{:S(2)}) copy-start(s32[2]{0:T(128)} %constant.116) | copy-start | bytes 28
  120.4 87.7 %copy-start.13 = (s32[2]{0:T(128)S(1)}, s32[2]{0:T(128)}, u32[]{:S(2)}) copy-start(s32[2]{0:T(128)} %constant.119) | copy-start | bytes 28
  203.8 105.5 %all-to-all-start.2 = ((f32[32,40,128]{2,1,0:T(8,128)}), f32[32,40,128]{2,1,0:T(8,128)S(1)}, u32[]{:S(2)}, u32[]{:S(2)}) async-start(f32[32,40,128]{2,1,0:T(8,128)} %bitcast.10), calls=%async_computation.2 | async-start | bytes 1310720 | tf_op jit(solution)/shard_map/all_to_all | solution.py:142
  207.7 159.4 %reduce-scatter.3.cloned.1.call-start = ((), (), s32[]{:S(2)}) async-start(), calls=%async_computation.8 | async-start | bytes 819200 | tf_op jit(solution)/shard_map/reduce_scatter | solution.py:156
  299.9 9.0 %copy-start.9 = (s32[32,40]{1,0:T(8,128)S(1)}, s32[32,40]{1,0:T(8,128)}, u32[]{:S(2)}) copy-start(s32[32,40]{1,0:T(8,128)} %param.21) | copy-start | bytes 15364
  299.9 9.1 %copy-start.10 = (s32[320,8]{0,1:T(8,128)S(1)}, s32[320,8]{0,1:T(8,128)}, u32[]{:S(2)}) copy-start(s32[320,8]{0,1:T(8,128)} %param.23) | copy-start | bytes 30724
  299.9 9.1 %copy-start.12 = (s32[2]{0:T(128)S(1)}, s32[2]{0:T(128)}, u32[]{:S(2)}) copy-start(s32[2]{0:T(128)} %constant.122) | copy-start | bytes 28
  299.9 9.2 %copy-start.11 = (s32[2]{0:T(128)S(1)}, s32[2]{0:T(128)}, u32[]{:S(2)}) copy-start(s32[2]{0:T(128)} %constant.125) | copy-start | bytes 28
  299.9 18.3 %copy-start.4 = (bf16[512,128]{1,0:T(8,128)(2,1)S(1)}, bf16[512,128]{1,0:T(8,128)(2,1)}, u32[]{:S(2)}) copy-start(bf16[512,128]{1,0:T(8,128)(2,1)} %param.18) | copy-start | bytes 393220
  300.0 20.0 %copy-start.15 = (bf16[512,128]{1,0:T(8,128)(2,1)S(1)}, bf16[512,128]{1,0:T(8,128)(2,1)}, u32[]{:S(2)}) copy-start(bf16[512,128]{1,0:T(8,128)(2,1)} %param.16) | copy-start | bytes 393220
  319.5 82.3 %reduce-scatter.5.cloned.1.call-start = ((), (), s32[]{:S(2)}) async-start(), calls=%async_computation.9 | async-start | bytes 819200 | tf_op jit(solution)/shard_map/reduce_scatter | solution.py:167
  344.0 22.8 %collective-permute-start = (bf16[160,128]{1,0:T(8,128)(2,1)S(1)}, bf16[160,128]{1,0:T(8,128)(2,1)S(1)}, u32[]{:S(2)}, u32[]{:S(2)}) collective-permute-start(bf16[160,128]{1,0:T(8,128)(2,1)S(1)} %get-tuple-element.36), channel_id=1, source_target_pairs={{0,4},{4,8},{8,12},{12,16},{16,20},{20,24},{24,28},{28,32},{32,36}... | collective-permute-start | bytes 122888 | tf_op jit(solution)/shard_map/ppermute | solution.py:19
  347.9 18.9 %collective-permute-start.1 = (bf16[160,128]{1,0:T(8,128)(2,1)S(1)}, bf16[160,128]{1,0:T(8,128)(2,1)S(1)}, u32[]{:S(2)}, u32[]{:S(2)}) collective-permute-start(bf16[160,128]{1,0:T(8,128)(2,1)S(1)} %get-tuple-element.37), channel_id=1, source_target_pairs={{4,0},{8,4},{12,8},{16,12},{20,16},{24,20},{28,24},{32,28},{36,32}... | collective-permute-start | bytes 122888 | tf_op jit(solution)/shard_map/ppermute | solution.py:21
  368.8 4.4 collective-permute-start.2
  370.6 3.9 collective-permute-start.3
  374.6 27.2 %copy-start.5 = (f32[320,128]{1,0:T(8,128)S(1)}, f32[320,128]{1,0:T(8,128)}, u32[]{:S(2)}) copy-start(f32[320,128]{1,0:T(8,128)} %reduce-scatter.3.cloned.1.call-done) | copy-start | bytes 491524
  375.9 114.4 %all-gather.5.cloned.1.call-start = ((), (), s32[]{:S(2)}) async-start(), calls=%async_computation.7 | async-start | bytes 10485760 | tf_op jit(solution)/shard_map/all_gather | solution.py:179
  389.4 22.5 %all-to-all-start.1 = ((bf16[32,40,128]{2,1,0:T(8,128)(2,1)}), bf16[32,40,128]{2,1,0:T(8,128)(2,1)S(1)}, u32[]{:S(2)}, u32[]{:S(2)}) async-start(bf16[32,40,128]{2,1,0:T(8,128)(2,1)} %bitcast.4), calls=%async_computation.1 | async-start | bytes 655360 | tf_op jit(solution)/shard_map/all_to_all | solution.py:130
  411.9 8.3 %copy-start.6 = (s32[32,256]{1,0:T(8,128)S(1)}, s32[32,256]{1,0:T(8,128)}, u32[]{:S(2)}) copy-start(s32[32,256]{1,0:T(8,128)} %param.19) | copy-start | bytes 98308
  411.9 207.6 %all-to-all-start.3 = ((f32[32,256,128]{2,1,0:T(8,128)}), f32[32,256,128]{2,1,0:T(8,128)}, u32[]{:S(2)}, u32[]{:S(2)}) async-start(f32[32,256,128]{2,1,0:T(8,128)} %bitcast.46), calls=%async_computation.5 | async-start | bytes 8388608 | tf_op jit(solution)/shard_map/all_to_all | solution.py:172
  420.1 317.5 %all-reduce.3.cloned.1.call-start = ((), (), s32[]{:S(2)}) async-start(), calls=%async_computation.10 | async-start | bytes 1572864 | tf_op jit(solution)/shard_map/psum | solution.py:182
  619.5 13.0 %copy-start.2 = (bf16[8192,128]{1,0:T(8,128)(2,1)S(1)}, bf16[8192,128]{1,0:T(8,128)(2,1)}, u32[]{:S(2)}) copy-start(bf16[8192,128]{1,0:T(8,128)(2,1)} %param.14) | copy-start | bytes 6291460
  632.5 110.2 %copy-start.1 = (bf16[512,128]{1,0:T(8,128)(2,1)S(1)}, bf16[512,128]{1,0:T(8,128)(2,1)}, u32[]{:S(2)}) copy-start(bf16[512,128]{1,0:T(8,128)(2,1)} %param.17) | copy-start | bytes 393220
Sparse Core Ops, SparseCore 0:
  75.3 85.3 all-gather.2
  319.6 23.6 reduce-scatter.2
  376.0 25.5 reduce-scatter.4
  403.1 87.0 all-gather.4
  632.6 105.0 all-reduce.2
where the time goes:
time: 756 us; the launch traced here: 749 us
  other arithmetic  254 us (34%)
  local copies, waits for them, and re-layouts  175 us (23%)
  waiting for transfers between devices  172 us (23%)
  blocking collectives  60.5 us (8%)
  matrix products  40 us (5%)
  starting transfers between devices  32.9 us (4%)
  between operations  14.5 us (2%)
    scatter-add x3, other arithmetic, spread_sum(): summed = summed.at[indices[:, column]].add(values)  128 us
    unnamed x9, other arithmetic  111 us
    psum x1, waiting for transfers between devices, local(): lax.psum((grad_encoder, grad_processor, grad_decoder), 'space')  99.7 us
    gather x3, local copies, waits for them, and re-layouts, gather_sum(): summed = summed + table[indices[:, column]].astype(jnp.float32)  88.3 us
    all_gather x1, waiting for transfers between devices, local(): grid_full = lax.all_gather(grid_state, 'chan', axis=1, tiled=True)  69.9 us
    gather x1, local copies, waits for them, and re-layouts, local(): sent_rows = grid_full[send_flat]  38.4 us
    all_to_all x1, blocking collectives, local(): lax.all_to_all(grid_state[g2m_send], 'space', split_axis=0, concat_axis=0...  37 us
    gather x1, local copies, waits for them, and re-layouts, local(): grid_state[g2m_send]  30.1 us
  transfers between devices with their start and end apart: 12, of which 4 were waited for; matrix products, arithmetic and copies ran while one was open for 56% of the time, Pallas kernels for 0%

commit v1 on v0

v1 whole, which is shorter than its diff:
```python
import functools

import jax
import jax.numpy as jnp
from jax import lax
from jax.experimental import pallas as pl
from jax.experimental.pallas import tpu as pltpu
from jax.sharding import PartitionSpec as P

REACH = 160
CHUNK = 512
MESH = pl.DeviceIdType.MESH
F32 = jnp.float32
BF16 = jnp.bfloat16


def dot(a, b):
    return jnp.dot(a, b, preferred_element_type=F32)


def dot_nt(a, b):
    return lax.dot_general(a, b, (((1,), (1,)), ((), ())), preferred_element_type=F32)


def dot_tn(a, b):
    return lax.dot_general(a, b, (((0,), (0,)), ((), ())), preferred_element_type=F32)


def slope(values):
    sigmoid = jax.nn.sigmoid(values)
    return sigmoid * (1.0 + values * (1.0 - sigmoid))


def row_iota(rows, lanes):
    return lax.broadcasted_iota(jnp.int32, (rows, lanes), 0).astype(F32).astype(BF16)


def ones_where(mask):
    return jnp.where(mask, jnp.ones((), BF16), jnp.zeros((), BF16))


def narrow(row, base):
    return (row - base).astype(F32).astype(BF16)


def kernel(
    sizes,
    grid_ref,
    cot_ref,
    we_ref,
    wp_ref,
    wd_ref,
    send_ref,
    key_ref,
    low_ref,
    mrow_ref,
    mcol_ref,
    edge_ref,
    rimt_ref,
    rim_ref,
    pred_ref,
    ge_ref,
    gp_ref,
    gd_ref,
    grid32,
    stage,
    sendbuf,
    recv,
    at,
    counts,
    slot_grad,
    back,
    sel,
    selt,
    rim,
    rimt,
    dgrad,
    second_part,
    second_recv,
    second,
    state_sum,
    state_full,
    gathered,
    first,
    first_full,
    ext,
    neighbour,
    mid_full,
    out_rows,
    slots,
    slots_t,
    rim_grad,
    halo_low,
    halo_high,
    proj_part,
    proj_recv,
    grads_a,
    grads_b,
    grecv_a,
    grecv_b,
    gout,
    ssem,
    rsem,
    gsem,
):
    ns, nc, fan, fan_m, fan_d = sizes
    me = lax.axis_index("space")
    my = lax.axis_index("chan")
    grid_rows, width = grid_ref.shape
    cap = send_ref.shape[1]
    mesh = state_sum.shape[0]
    cap2 = back.shape[1]
    heads = counts.shape[0]
    per = cap // 128
    reach = halo_low.shape[0]
    share = grads_b.shape[1]
    fan_scale = fan ** (-0.5)
    fan_m_scale = fan_m ** (-0.5)
    fan_d_scale = fan_d ** (-0.5)
    all_slots = ns * cap2
    nxt = lax.rem(me + 1, ns)
    prv = lax.rem(me + ns - 1, ns)

    def remote(src, dst, which, space, chan, rec=None):
        return pltpu.make_async_remote_copy(
            src_ref=src,
            dst_ref=dst,
            send_sem=ssem.at[which],
            recv_sem=rsem.at[which] if rec is None else rec,
            device_id=(space, chan),
            device_id_type=MESH,
        )

    def peers(body):
        def step(k, carry):
            body(lax.rem(me + k, ns))
            return carry

        lax.fori_loop(1, ns, step, 0)

    def chans(body):
        for k in range(1, nc):
            body(lax.rem(my + k, nc))

    def wait_chan(buf, which):
        part = buf.at[pl.ds(0, nc - 1)]
        remote(part, part, which, me, my).wait_recv()

    def wait_space(buf, which):
        part = buf.at[pl.ds(0, ns - 1)]
        remote(part, part, which, me, my).wait_recv()

    def sent(buf, count, which):
        part = buf.at[pl.ds(0, count)]
        remote(part, part, which, me, my).wait_send()

    barrier = pltpu.get_barrier_semaphore()

    def greet(peer):
        pl.semaphore_signal(barrier, inc=1, device_id=(peer, my), device_id_type=MESH)

    peers(greet)

    def greet_chan(c):
        pl.semaphore_signal(barrier, inc=1, device_id=(me, c), device_id_type=MESH)

    chans(greet_chan)

    def widen(i, carry):
        rows = pl.ds(pl.multiple_of(i * CHUNK, CHUNK), CHUNK)
        grid32[rows, :] = grid_ref[rows, :].astype(F32)
        return carry

    lax.fori_loop(0, grid_rows // CHUNK, widen, 0)
    pl.semaphore_wait(barrier, ns + nc - 2)

    def pick(peer):
        def some(i, carry):
            base = pl.multiple_of(i * 16, 16)
            for u in range(16):
                stage[pl.ds(base + u, 1), :] = grid32[pl.ds(send_ref[peer, base + u], 1), :]
            return carry

        lax.fori_loop(0, cap // 16, some, 0)

    def pick_and_send(peer):
        pick(peer)
        sendbuf[peer] = stage[...].astype(BF16)
        remote(sendbuf.at[peer], recv.at[me], 0, peer, my, gsem.at[me]).start()

    peers(pick_and_send)
    pick(me)
    recv[me] = stage[...].astype(BF16)

    iota = row_iota(128, 128)
    slot_grad[...] = jnp.zeros(slot_grad.shape, F32)

    def edge_step(i, carry):
        start = pl.multiple_of(i * CHUNK, CHUNK)
        rows = edge_ref[:, pl.ds(start, CHUNK)]
        for kb in range(all_slots // 128):
            cut = [narrow(rows[j : j + 1, :], kb * 128) for j in range(fan_d)]
            for lb in range(CHUNK // 128):
                total = None
                for j in range(fan_d):
                    one = ones_where(iota == cut[j][:, lb * 128 : (lb + 1) * 128])
                    total = one if total is None else total + one
                at[kb * 128 : (kb + 1) * 128, pl.ds(start + lb * 128, 128)] = total
        slot_grad[...] += dot(at[:, pl.ds(start, CHUNK)], cot_ref[pl.ds(start, CHUNK), :])
        return carry

    lax.fori_loop(0, grid_rows // CHUNK, edge_step, 0)
    slot_grad[...] = slot_grad[...] * fan_d_scale
    own_rows = pl.ds(pl.multiple_of(me * cap2, cap2), cap2)

    def send_back(peer):
        rows = pl.ds(pl.multiple_of(peer * cap2, cap2), cap2)
        remote(slot_grad.at[rows], back.at[me], 1, peer, my).start()

    peers(send_back)
    back[me] = slot_grad[own_rows, :]

    def count_step(g, carry):
        key = key_ref[pl.ds(g, 1), :]
        low = low_ref[pl.ds(g, 1), :]
        lanes = key.shape[1]
        big = row_iota(128, lanes)
        right = ones_where(big == narrow(low, 0))
        for kb in range(heads * 8 // 128):
            left = ones_where(big == narrow(key, kb * 128))
            counts[kb * 16 : (kb + 1) * 16, pl.ds(pl.multiple_of(g * 8, 8), 8), :] = dot_nt(
                left, right
            ).reshape(16, 8, 128)
        return carry

    lax.fori_loop(0, mesh // 8, count_step, 0)

    rows_iota = lax.broadcasted_iota(jnp.int32, (rimt.shape[0], mesh), 0)
    lane_iota = lax.broadcasted_iota(jnp.int32, (mesh, rim.shape[1]), 1)
    total_t = jnp.zeros(rimt.shape, F32)
    total = jnp.zeros(rim.shape, F32)
    for j in range(fan_m):
        total_t = total_t + jnp.where(rows_iota == rimt_ref[j : j + 1, :], 1.0, 0.0)
        total = total + jnp.where(lane_iota == rim_ref[:, j : j + 1], 1.0, 0.0)
    rimt[...] = total_t.astype(BF16)
    rim[...] = total.astype(BF16)
    selt[...] = jnp.where(
        lax.broadcasted_iota(jnp.int32, selt.shape, 0) == mrow_ref[...], 1.0, 0.0
    ).astype(BF16)
    sel[...] = jnp.where(
        lax.broadcasted_iota(jnp.int32, sel.shape, 1) == mcol_ref[...], 1.0, 0.0
    ).astype(BF16)

    wait_space(back, 1)
    dgrad[...] = dot(selt[...], back[...].reshape(all_slots, width).astype(BF16)).astype(BF16)
    for c in range(nc):
        second_part[c] = dot_nt(dgrad[...], wd_ref[c * width : (c + 1) * width, :]).astype(BF16)

    def send_second(c):
        remote(second_part.at[c], second_recv.at[my], 2, me, c).start()

    chans(send_second)
    second_recv[my] = second_part[my]

    def absorb(source):
        left = jnp.concatenate([counts[source * per + h] for h in range(per)], axis=1)
        return dot(left.astype(BF16), recv[source])

    state_sum[...] = absorb(me)

    def absorb_step(k, carry):
        source = lax.rem(me + ns - k, ns)
        remote(recv.at[source], recv.at[source], 0, me, my, gsem.at[source]).wait_recv()
        state_sum[...] += absorb(source)
        return carry

    lax.fori_loop(1, ns, absorb_step, 0)
    state_full[my] = state_sum[...].astype(BF16)

    def send_state(c):
        remote(state_full.at[my], state_full.at[my], 3, me, c).start()

    chans(send_state)

    wait_chan(second_recv, 2)
    total = second_recv[0].astype(F32)
    for c in range(1, nc):
        total = total + second_recv[c].astype(F32)
    second[...] = total

    wait_chan(state_full, 3)
    total = dot(state_full[0], we_ref[0:width, :])
    for c in range(1, nc):
        total = total + dot(state_full[c], we_ref[c * width : (c + 1) * width, :])
    total = total * fan_scale
    gathered[...] = total
    first_full[my] = (total * jax.nn.sigmoid(total)).astype(BF16)

    def send_first(c):
        remote(first_full.at[my], first_full.at[my], 4, me, c).start()

    chans(send_first)
    first[...] = first_full[my].astype(F32)
    wait_chan(first_full, 4)
    total = dot(first_full[0], wp_ref[0:width, :])
    for c in range(1, nc):
        total = total + dot(first_full[c], wp_ref[c * width : (c + 1) * width, :])
    ext[reach : reach + mesh, :] = total.astype(BF16)
    to_next = remote(
        ext.at[pl.ds(mesh, reach)], ext.at[pl.ds(0, reach)], 5, nxt, my
    )
    to_prev = remote(
        ext.at[pl.ds(reach, reach)], ext.at[pl.ds(reach + mesh, reach)], 6, prv, my
    )
    to_next.start()
    to_prev.start()
    to_next.wait()
    to_prev.wait()
    total = dot(rim[...], ext[...]) * fan_m_scale
    neighbour[...] = total
    mid_full[my] = (first[...] + total * jax.nn.sigmoid(total)).astype(BF16)

    def send_mid(c):
        remote(mid_full.at[my], mid_full.at[my], 7, me, c).start()

    chans(send_mid)
    pre = (second[...] * slope(neighbour[...]) * fan_m_scale).astype(BF16)
    rim_grad[...] = dot(rimt[...], pre)
    down = remote(rim_grad.at[pl.ds(0, reach)], halo_high, 8, prv, my)
    up = remote(rim_grad.at[pl.ds(reach + mesh, reach)], halo_low, 9, nxt, my)
    down.start()
    up.start()

    wait_chan(mid_full, 7)
    total = dot(mid_full[0], wd_ref[0:width, :])
    for c in range(1, nc):
        total = total + dot(mid_full[c], wd_ref[c * width : (c + 1) * width, :])
    out_rows[...] = dot(sel[...], total.astype(BF16)).reshape(out_rows.shape)

    def send_rows(peer):
        remote(out_rows.at[peer], slots.at[me], 10, peer, my).start()

    peers(send_rows)
    slots[me] = out_rows[me]

    down.wait()
    up.wait()
    rim_grad[reach : 2 * reach, :] += halo_low[...]
    rim_grad[mesh : mesh + reach, :] += halo_high[...]
    projected = rim_grad[reach : reach + mesh, :].astype(BF16)
    for c in range(nc):
        proj_part[c] = dot_nt(projected, wp_ref[c * width : (c + 1) * width, :]).astype(BF16)

    def send_proj(c):
        remote(proj_part.at[c], proj_recv.at[my], 11, me, c).start()

    chans(send_proj)
    proj_recv[my] = proj_part[my]
    blocks = width // share
    for c in range(nc):
        cut = slice(c * blocks, (c + 1) * blocks)
        grads_a[cut, 0:share, :] = (
            dot_tn(mid_full[c], dgrad[...]).astype(BF16).reshape(blocks, share, width)
        )
        grads_a[cut, share : 2 * share, :] = (
            dot_tn(first_full[c], projected).astype(BF16).reshape(blocks, share, width)
        )

    def send_a(peer):
        remote(grads_a.at[peer], grecv_a.at[me], 12, peer, my).start()

    peers(send_a)
    grecv_a[me] = grads_a[me]

    wait_chan(proj_recv, 11)
    total = second[...]
    for c in range(nc):
        total = total + proj_recv[c].astype(F32)
    sum_grad = (total * slope(gathered[...]) * fan_scale).astype(BF16)
    for c in range(nc):
        cut = slice(c * blocks, (c + 1) * blocks)
        grads_b[cut] = (
            dot_tn(state_full[c], sum_grad).astype(BF16).reshape(blocks, share, width)
        )

    def send_b(peer):
        remote(grads_b.at[peer], grecv_b.at[me], 13, peer, my).start()

    peers(send_b)
    grecv_b[me] = grads_b[me]

    wait_space(slots, 10)
    slots_t[...] = slots[...].reshape(all_slots, width).T.astype(BF16)

    def predict(i, carry):
        start = pl.multiple_of(i * CHUNK, CHUNK)
        moved = dot(slots_t[...], at[:, pl.ds(start, CHUNK)]) * fan_d_scale
        rows = pl.ds(start, CHUNK)
        pred_ref[rows, :] = (grid_ref[rows, :].astype(F32) + moved.T).astype(BF16)
        return carry

    steps = grid_rows // CHUNK
    lax.fori_loop(0, steps // 2, predict, 0)

    wait_space(grecv_a, 12)
    wait_space(grecv_b, 13)
    total_a = grecv_a[0].astype(F32)
    total_b = grecv_b[0].astype(F32)
    for s in range(1, ns):
        total_a = total_a + grecv_a[s].astype(F32)
        total_b = total_b + grecv_b[s].astype(F32)
    gout[me, 0 : 2 * share, :] = total_a.astype(BF16)
    gout[me, 2 * share : 3 * share, :] = total_b.astype(BF16)

    def send_out(peer):
        remote(gout.at[me], gout.at[me], 14, peer, my).start()

    peers(send_out)
    lax.fori_loop(steps // 2, steps, predict, 0)
    wait_space(gout, 14)
    whole = gout[...].astype(F32)
    gd_ref[...] = whole[:, 0:share, :].reshape(gd_ref.shape)
    gp_ref[...] = whole[:, share : 2 * share, :].reshape(gp_ref.shape)
    ge_ref[...] = whole[:, 2 * share : 3 * share, :].reshape(ge_ref.shape)

    sent(sendbuf, ns - 1, 0)
    sent(back, ns - 1, 1)
    sent(second_part, nc - 1, 2)
    sent(state_full, nc - 1, 3)
    sent(first_full, nc - 1, 4)
    sent(mid_full, nc - 1, 7)
    sent(out_rows, ns - 1, 10)
    sent(proj_part, nc - 1, 11)
    sent(grads_a, ns - 1, 12)
    sent(grads_b, ns - 1, 13)
    sent(gout, ns - 1, 14)


def local(
    grid_state,
    cotangent,
    encoder_weight,
    processor_weight,
    decoder_weight,
    g2m_send,
    g2m_edges,
    m2g_send,
    m2g_edges,
    m2m_edges,
):
    ns = lax.axis_size("space")
    nc = lax.axis_size("chan")
    me = lax.axis_index("space")
    grid_rows, width = grid_state.shape
    mesh, fan = g2m_edges.shape
    fan_m = m2m_edges.shape[1]
    fan_d = m2g_edges.shape[1]
    cap = g2m_send.shape[1]
    cap2 = m2g_send.shape[1]
    reach = min(REACH, mesh // 2)
    full = encoder_weight.shape[0]
    share = full // ns
    heads = ns * cap // 128

    node = lax.broadcasted_iota(jnp.int32, g2m_edges.shape, 0)
    key = ((g2m_edges // 128) * 8 + node % 8).reshape(mesh // 8, 8 * fan)
    low = (g2m_edges % 128).reshape(mesh // 8, 8 * fan)
    rows = lax.broadcasted_iota(jnp.int32, (fan_m, mesh), 1)
    rim_t = (m2m_edges.T - me * mesh - rows + reach) % (ns * mesh) + rows
    rim = rim_t.T
    flat = m2g_send.reshape(1, ns * cap2)

    vmem = pl.BlockSpec(memory_space=pltpu.VMEM)
    smem = pl.BlockSpec(memory_space=pltpu.SMEM)
    weight = jax.ShapeDtypeStruct((full, width), F32)
    return tuple(
        pl.pallas_call(
            functools.partial(kernel, (ns, nc, fan, fan_m, fan_d)),
            out_shape=(
                jax.ShapeDtypeStruct(grid_state.shape, BF16),
                weight,
                weight,
                weight,
            ),
            in_specs=[vmem] * 5 + [smem] + [vmem] * 7,
            out_specs=(vmem,) * 4,
            scratch_shapes=[
                pltpu.VMEM((grid_rows, width), F32),
                pltpu.VMEM((cap, width), F32),
                pltpu.VMEM((ns, cap, width), BF16),
                pltpu.VMEM((ns, cap, width), BF16),
                pltpu.VMEM((ns * cap2, grid_rows), BF16),
                pltpu.VMEM((heads, mesh, 128), F32),
                pltpu.VMEM((ns * cap2, width), F32),
                pltpu.VMEM((ns, cap2, width), F32),
                pltpu.VMEM((ns * cap2, mesh), BF16),
                pltpu.VMEM((mesh, ns * cap2), BF16),
                pltpu.VMEM((mesh, mesh + 2 * reach), BF16),
                pltpu.VMEM((mesh + 2 * reach, mesh), BF16),
                pltpu.VMEM((mesh, width), BF16),
                pltpu.VMEM((nc, mesh, width), BF16),
                pltpu.VMEM((nc, mesh, width), BF16),
                pltpu.VMEM((mesh, width), F32),
                pltpu.VMEM((mesh, width), F32),
                pltpu.VMEM((nc, mesh, width), BF16),
                pltpu.VMEM((mesh, width), F32),
                pltpu.VMEM((mesh, width), F32),
                pltpu.VMEM((nc, mesh, width), BF16),
                pltpu.VMEM((mesh + 2 * reach, width), BF16),
                pltpu.VMEM((mesh, width), F32),
                pltpu.VMEM((nc, mesh, width), BF16),
                pltpu.VMEM((ns, cap2, width), F32),
                pltpu.VMEM((ns, cap2, width), F32),
                pltpu.VMEM((width, ns * cap2), BF16),
                pltpu.VMEM((mesh + 2 * reach, width), F32),
                pltpu.VMEM((reach, width), F32),
                pltpu.VMEM((reach, width), F32),
                pltpu.VMEM((nc, mesh, width), BF16),
                pltpu.VMEM((nc, mesh, width), BF16),
                pltpu.VMEM((ns, 2 * share, width), BF16),
                pltpu.VMEM((ns, share, width), BF16),
                pltpu.VMEM((ns, 2 * share, width), BF16),
                pltpu.VMEM((ns, share, width), BF16),
                pltpu.VMEM((ns, 3 * share, width), BF16),
                pltpu.SemaphoreType.DMA((15,)),
                pltpu.SemaphoreType.DMA((15,)),
                pltpu.SemaphoreType.DMA((ns,)),
            ],
            compiler_params=pltpu.CompilerParams(
                collective_id=0,
                has_side_effects=True,
                vmem_limit_bytes=62 * 1024 * 1024,
            ),
            cost_estimate=pl.CostEstimate(
                flops=12_000_000_000, bytes_accessed=10_000_000, transcendentals=0
            ),
            name="encode_process_decode",
        )(
            grid_state,
            cotangent,
            encoder_weight,
            processor_weight,
            decoder_weight,
            g2m_send,
            key,
            low,
            flat,
            flat.reshape(ns * cap2, 1),
            m2g_edges.T,
            rim_t,
            rim,
        )
    )


def solution(mesh):
    placed = (P("space", "chan"),) * 2 + (P(None, "chan"),) * 3 + (P("space", None),) * 5
    return jax.shard_map(
        local,
        mesh=mesh,
        in_specs=placed,
        out_specs=(P("space", "chan"),) + (P(None, "chan"),) * 3,
        check_vma=False,
    )
```

time: 756 us -> 137 us (0.18)
  other arithmetic: 254 us -> 3.11 us
  waiting for transfers between devices: 172 us -> 0 us
  local copies, waits for them, and re-layouts: 175 us -> 9.75 us
  Pallas kernels: 0 us -> 124 us
  blocking collectives: 60.5 us -> 0 us
  matrix products: 40 us -> 0 us
  starting transfers between devices: 32.9 us -> 0 us
  between operations: 14.5 us -> 0.74 us
    gather x6 -> x0, local copies, waits for them, and re-layouts: 160 us -> none  [the longest x3 88.3 us: gather_sum(): summed = summed + table[indices[:, column]].astype(jnp.float32)]
    scatter-add x6 -> x0, other arithmetic: 137 us -> none  [the longest x3 128 us: spread_sum(): summed = summed.at[indices[:, column]].add(values)]
    pallas_call x0 -> x1, Pallas kernels: none -> 124 us  [local(): pl.pallas_call(functools.partial(kernel, (ns, nc, fan, fan_m, fan_d)), ou...]
    unnamed x9 -> x0, other arithmetic: 111 us -> none
    psum x1 -> x0, waiting for transfers between devices: 99.7 us -> none  [local(): lax.psum((grad_encoder, grad_processor, grad_decoder), 'space')]
    all_gather x2 -> x0, waiting for transfers between devices: 69.9 us -> none  [the longest x1 69.9 us: local(): grid_full = lax.all_gather(grid_state, 'chan', axis=1, tiled=True)]
    dot_general x11 -> x0, matrix products: 40 us -> none  [the longest x5 27.3 us: lead_dot(): lax.dot_general(left.astype(jnp.float32), right, (((0,), (0,)), ((), ()))...]
    all_to_all x1 -> x0, blocking collectives: 37 us -> none  [local(): lax.all_to_all(grid_state[g2m_send], 'space', split_axis=0, concat_axis=0...]
  transfers between devices with their start and end apart: 12 -> 0, of which waited for: 4 -> 0; matrix products, arithmetic and copies ran while one was open for 56% -> 0% of each run, Pallas kernels for 0% -> 0%
where the time goes in v1:
time: 137 us
  Pallas kernels  124 us (91%)
  local copies, waits for them, and re-layouts  9.75 us (7%)
  other arithmetic  3.11 us (2%)
    pallas_call x1, Pallas kernels, local(): pl.pallas_call(functools.partial(kernel, (ns, nc, fan, fan_m, fan_d)), ou...  124 us
    unnamed x12, local copies, waits for them, and re-layouts  5.24 us

profile of v1, /device:TPU:1, one launch (start us, length us, event | category | flops | bytes accessed | tf_op | source)
XLA Modules:
  0.0 137.2 jit_solution(11888384773756031692)
XLA Ops:
  0.6 0.0 copy-start.3
  0.7 1.4 %reshape.19.mrow_ref = s32[1,1280]{1,0:T(1,128)} reshape(s32[32,40]{1,0:T(8,128)} %param.17) | data formatting | bytes 10240 | tf_op jit(solution)/shard_map/reshape | solution.py:471
  2.1 0.7 subtract_add_fusion
  2.8 0.9 add_select_fusion.2
  3.7 0.1 copy.30
  3.8 0.7 reshape.18.low_ref
  4.6 0.1 copy.33
  4.7 0.8 fusion.rim_ref
  5.5 0.1 copy.29
  5.6 0.7 reshape.17.key_ref
  6.3 0.1 copy.31
  6.4 0.1 add_select_fusion.1
  6.6 0.1 copy.32
  6.6 0.6 iota_add_fusion.rimt_ref
  7.3 0.0 copy-done.3
  7.3 1.1 reshape_reshape.4.mcol_ref
  8.3 123.6 %encode_process_decode.1 = (bf16[8192,128]{1,0:T(8,128)(2,1)}, f32[512,128]{1,0:T(8,128)}, f32[512,128]{1,0:T(8,128)}, f32[512,128]{1,0:T(8,128)}) custom-call(bf16[8192,128]{1,0:T(8,128)(2,1)} %grid_ref.1, bf16[8192,128]{1,0:T(8,128)(2,1)} %cot_ref.1, bf16[512,128]{1,0:T(8,128)(2,1)} %we_ref.1, bf16[512,128]{1,0:T(8,128)(2,1)} %wp_ref.1, ...), custom_call_target="tpu_custom_call" | custom-call | flops 12000000000 | bytes 10000000 | tf_op jit(solution)/shard_map/encode_process_decode/pallas_call | solution.py:477
  131.9 0.0 copy-start.2
  131.9 0.0 copy-start.1
  131.9 0.0 copy-start
  131.9 3.1 %copy.41 = bf16[8192,128]{1,0:T(8,128)(2,1)} copy(bf16[8192,128]{1,0:T(8,128)(2,1)} %get-tuple-element.14) | data formatting | bytes 4194304
  135.0 0.0 copy-done.2
  135.0 0.7 copy.42
  135.7 0.0 copy-done.1
  135.8 0.7 copy.43
  136.5 0.0 copy-done
  136.5 0.7 copy.44
  (2 shorter events, 0.0 us)
Async XLA Ops:
  0.6 6.6 %copy-start.3 = (s32[32,40]{1,0:T(8,128)S(1)}, s32[32,40]{1,0:T(8,128)}, u32[]{:S(2)}) copy-start(s32[32,40]{1,0:T(8,128)} %param.17) | copy-start | bytes 15364
  131.9 3.1 %copy-start.2 = (f32[512,128]{1,0:T(8,128)S(1)}, f32[512,128]{1,0:T(8,128)}, u32[]{:S(2)}) copy-start(f32[512,128]{1,0:T(8,128)} %get-tuple-element.15) | copy-start | bytes 786436
  131.9 3.8 %copy-start.1 = (f32[512,128]{1,0:T(8,128)S(1)}, f32[512,128]{1,0:T(8,128)}, u32[]{:S(2)}) copy-start(f32[512,128]{1,0:T(8,128)} %get-tuple-element.16) | copy-start | bytes 786436
  131.9 4.5 %copy-start = (f32[512,128]{1,0:T(8,128)S(1)}, f32[512,128]{1,0:T(8,128)}, u32[]{:S(2)}) copy-start(f32[512,128]{1,0:T(8,128)} %get-tuple-element.17) | copy-start | bytes 786436

commit v2 on v1

--- a/solution.py
+++ b/solution.py
@@ -8,7 +8,7 @@
 from jax.sharding import PartitionSpec as P
 
 REACH = 160
-CHUNK = 512
+CHUNK = 1024
 MESH = pl.DeviceIdType.MESH
 F32 = jnp.float32
 BF16 = jnp.bfloat16
@@ -51,13 +51,10 @@
     wp_ref,
     wd_ref,
     send_ref,
-    key_ref,
-    low_ref,
-    mrow_ref,
-    mcol_ref,
+    source_ref,
+    mesh_send_ref,
     edge_ref,
-    rimt_ref,
-    rim_ref,
+    near_ref,
     pred_ref,
     ge_ref,
     gp_ref,
@@ -66,10 +63,14 @@
     stage,
     sendbuf,
     recv,
-    at,
+    at_even,
+    at_odd,
+    key,
+    low,
     counts,
     slot_grad,
     back,
+    sel32,
     sel,
     selt,
     rim,
@@ -176,12 +177,13 @@
 
     def pick(peer):
         def some(i, carry):
-            base = pl.multiple_of(i * 16, 16)
-            for u in range(16):
-                stage[pl.ds(base + u, 1), :] = grid32[pl.ds(send_ref[peer, base + u], 1), :]
+            base = pl.multiple_of(i * 32, 32)
+            rows = [grid32[pl.ds(send_ref[peer, base + u], 1), :] for u in range(32)]
+            for u in range(32):
+                stage[pl.ds(base + u, 1), :] = rows[u]
             return carry
 
-        lax.fori_loop(0, cap // 16, some, 0)
+        lax.fori_loop(0, cap // 32, some, 0)
 
     def pick_and_send(peer):
         pick(peer)
@@ -195,21 +197,43 @@
     iota = row_iota(128, 128)
     slot_grad[...] = jnp.zeros(slot_grad.shape, F32)
 
-    def edge_step(i, carry):
-        start = pl.multiple_of(i * CHUNK, CHUNK)
+    steps = grid_rows // CHUNK
+    half = all_slots // 2
+
+    def build(buf, at, step, lo, hi):
+        start = pl.multiple_of(step * CHUNK, CHUNK)
         rows = edge_ref[:, pl.ds(start, CHUNK)]
-        for kb in range(all_slots // 128):
+        for kb in range(lo // 128, hi // 128):
             cut = [narrow(rows[j : j + 1, :], kb * 128) for j in range(fan_d)]
             for lb in range(CHUNK // 128):
                 total = None
                 for j in range(fan_d):
                     one = ones_where(iota == cut[j][:, lb * 128 : (lb + 1) * 128])
                     total = one if total is None else total + one
-                at[kb * 128 : (kb + 1) * 128, pl.ds(start + lb * 128, 128)] = total
-        slot_grad[...] += dot(at[:, pl.ds(start, CHUNK)], cot_ref[pl.ds(start, CHUNK), :])
+                buf[at, kb * 128 : (kb + 1) * 128, lb * 128 : (lb + 1) * 128] = total
+
+    def spread(buf, at, step, lo, hi):
+        rows = pl.ds(pl.multiple_of(step * CHUNK, CHUNK), CHUNK)
+        slot_grad[lo:hi, :] += dot(buf[at, lo:hi, :], cot_ref[rows, :])
+
+    cuts = [(0, half), (half, all_slots)] if half % 128 == 0 else [(0, all_slots)]
+    build(at_even, 0, 0, 0, all_slots)
+
+    def edge_step(t, carry):
+        for lo, hi in cuts:
+            spread(at_even, t, 2 * t, lo, hi)
+            build(at_odd, t, 2 * t + 1, lo, hi)
+        for lo, hi in cuts:
+            spread(at_odd, t, 2 * t + 1, lo, hi)
+            build(at_even, t + 1, 2 * t + 2, lo, hi)
         return carry
 
-    lax.fori_loop(0, grid_rows // CHUNK, edge_step, 0)
+    last = steps // 2 - 1
+    lax.fori_loop(0, last, edge_step, 0)
+    for lo, hi in cuts:
+        spread(at_even, last, 2 * last, lo, hi)
+        build(at_odd, last, 2 * last + 1, lo, hi)
+    spread(at_odd, last, 2 * last + 1, 0, all_slots)
     slot_grad[...] = slot_grad[...] * fan_d_scale
     own_rows = pl.ds(pl.multiple_of(me * cap2, cap2), cap2)
 
@@ -220,36 +244,48 @@
     peers(send_back)
     back[me] = slot_grad[own_rows, :]
 
+    octets = mesh // 8
+    parts = [source_ref[pl.ds(u, octets, stride=8), :] for u in range(8)]
+    key[...] = jnp.concatenate([(part // 128) * 8 + u for u, part in enumerate(parts)], axis=1)
+    low[...] = jnp.concatenate([part % 128 for part in parts], axis=1)
+    big = row_iota(128, key.shape[1])
+
     def count_step(g, carry):
-        key = key_ref[pl.ds(g, 1), :]
-        low = low_ref[pl.ds(g, 1), :]
-        lanes = key.shape[1]
-        big = row_iota(128, lanes)
-        right = ones_where(big == narrow(low, 0))
+        found = []
+        for u in range(2):
+            top = key[pl.ds(2 * g + u, 1), :]
+            right = ones_where(big == narrow(low[pl.ds(2 * g + u, 1), :], 0))
+            found.append(
+                [
+                    dot_nt(ones_where(big == narrow(top, kb * 128)), right).reshape(16, 8, 128)
+                    for kb in range(heads * 8 // 128)
+                ]
+            )
+        rows = pl.ds(pl.multiple_of(g * 16, 16), 16)
         for kb in range(heads * 8 // 128):
-            left = ones_where(big == narrow(key, kb * 128))
-            counts[kb * 16 : (kb + 1) * 16, pl.ds(pl.multiple_of(g * 8, 8), 8), :] = dot_nt(
-                left, right
-            ).reshape(16, 8, 128)
+            pair = jnp.concatenate([found[0][kb], found[1][kb]], axis=1)
+            counts[kb * 16 : (kb + 1) * 16, rows, :] = pair.astype(BF16)
         return carry
 
-    lax.fori_loop(0, mesh // 8, count_step, 0)
-
-    rows_iota = lax.broadcasted_iota(jnp.int32, (rimt.shape[0], mesh), 0)
-    lane_iota = lax.broadcasted_iota(jnp.int32, (mesh, rim.shape[1]), 1)
-    total_t = jnp.zeros(rimt.shape, F32)
-    total = jnp.zeros(rim.shape, F32)
+    lax.fori_loop(0, mesh // 16, count_step, 0, unroll=2)
+
+    node = lax.broadcasted_iota(jnp.int32, near_ref.shape, 1)
+    span = ns * mesh
+    offset = near_ref[...] - me * mesh - node + reach
+    offset = jnp.where(offset < 0, offset + span, offset)
+    offset = jnp.where(offset >= span, offset - span, offset) + node
+    rows_iota = lax.broadcasted_iota(jnp.int32, rimt.shape, 0)
+    total = jnp.zeros(rimt.shape, F32)
     for j in range(fan_m):
-        total_t = total_t + jnp.where(rows_iota == rimt_ref[j : j + 1, :], 1.0, 0.0)
-        total = total + jnp.where(lane_iota == rim_ref[:, j : j + 1], 1.0, 0.0)
-    rimt[...] = total_t.astype(BF16)
-    rim[...] = total.astype(BF16)
-    selt[...] = jnp.where(
-        lax.broadcasted_iota(jnp.int32, selt.shape, 0) == mrow_ref[...], 1.0, 0.0
-    ).astype(BF16)
-    sel[...] = jnp.where(
-        lax.broadcasted_iota(jnp.int32, sel.shape, 1) == mcol_ref[...], 1.0, 0.0
-    ).astype(BF16)
+        total = total + jnp.where(rows_iota == offset[j : j + 1, :], 1.0, 0.0)
+    rimt[...] = total.astype(BF16)
+    rim[...] = total.T.astype(BF16)
+    lane_iota = lax.broadcasted_iota(jnp.int32, (cap2, mesh), 1)
+    for p in range(ns):
+        column = mesh_send_ref[:, p : p + 1]
+        sel32[p * cap2 : (p + 1) * cap2, :] = jnp.where(lane_iota == column, 1.0, 0.0)
+    sel[...] = sel32[...].astype(BF16)
+    selt[...] = sel32[...].T.astype(BF16)
 
     wait_space(back, 1)
     dgrad[...] = dot(selt[...], back[...].reshape(all_slots, width).astype(BF16)).astype(BF16)
@@ -264,7 +300,7 @@
 
     def absorb(source):
         left = jnp.concatenate([counts[source * per + h] for h in range(per)], axis=1)
-        return dot(left.astype(BF16), recv[source])
+        return dot(left, recv[source])
 
     state_sum[...] = absorb(me)
 
@@ -392,15 +428,14 @@
     wait_space(slots, 10)
     slots_t[...] = slots[...].reshape(all_slots, width).T.astype(BF16)
 
-    def predict(i, carry):
-        start = pl.multiple_of(i * CHUNK, CHUNK)
-        moved = dot(slots_t[...], at[:, pl.ds(start, CHUNK)]) * fan_d_scale
-        rows = pl.ds(start, CHUNK)
-        pred_ref[rows, :] = (grid_ref[rows, :].astype(F32) + moved.T).astype(BF16)
+    def predict(t, carry):
+        for u, buf in enumerate((at_even, at_odd)):
+            moved = dot(slots_t[...], buf[t]) * fan_d_scale
+            rows = pl.ds(pl.multiple_of((2 * t + u) * CHUNK, CHUNK), CHUNK)
+            pred_ref[rows, :] = (grid_ref[rows, :].astype(F32) + moved.T).astype(BF16)
         return carry
 
-    steps = grid_rows // CHUNK
-    lax.fori_loop(0, steps // 2, predict, 0)
+    lax.fori_loop(0, steps // 4, predict, 0)
 
     wait_space(grecv_a, 12)
     wait_space(grecv_b, 13)
@@ -416,7 +451,7 @@
         remote(gout.at[me], gout.at[me], 14, peer, my).start()
 
     peers(send_out)
-    lax.fori_loop(steps // 2, steps, predict, 0)
+    lax.fori_loop(steps // 4, steps // 2, predict, 0)
     wait_space(gout, 14)
     whole = gout[...].astype(F32)
     gd_ref[...] = whole[:, 0:share, :].reshape(gd_ref.shape)
@@ -450,7 +485,6 @@
 ):
     ns = lax.axis_size("space")
     nc = lax.axis_size("chan")
-    me = lax.axis_index("space")
     grid_rows, width = grid_state.shape
     mesh, fan = g2m_edges.shape
     fan_m = m2m_edges.shape[1]
@@ -461,14 +495,7 @@
     full = encoder_weight.shape[0]
     share = full // ns
     heads = ns * cap // 128
-
-    node = lax.broadcasted_iota(jnp.int32, g2m_edges.shape, 0)
-    key = ((g2m_edges // 128) * 8 + node % 8).reshape(mesh // 8, 8 * fan)
-    low = (g2m_edges % 128).reshape(mesh // 8, 8 * fan)
-    rows = lax.broadcasted_iota(jnp.int32, (fan_m, mesh), 1)
-    rim_t = (m2m_edges.T - me * mesh - rows + reach) % (ns * mesh) + rows
-    rim = rim_t.T
-    flat = m2g_send.reshape(1, ns * cap2)
+    halves = grid_rows // CHUNK // 2
 
     vmem = pl.BlockSpec(memory_space=pltpu.VMEM)
     smem = pl.BlockSpec(memory_space=pltpu.SMEM)
@@ -482,17 +509,21 @@
                 weight,
                 weight,
             ),
-            in_specs=[vmem] * 5 + [smem] + [vmem] * 7,
+            in_specs=[vmem] * 5 + [smem] + [vmem] * 4,
             out_specs=(vmem,) * 4,
             scratch_shapes=[
                 pltpu.VMEM((grid_rows, width), F32),
                 pltpu.VMEM((cap, width), F32),
                 pltpu.VMEM((ns, cap, width), BF16),
                 pltpu.VMEM((ns, cap, width), BF16),
-                pltpu.VMEM((ns * cap2, grid_rows), BF16),
-                pltpu.VMEM((heads, mesh, 128), F32),
+                pltpu.VMEM((halves, ns * cap2, CHUNK), BF16),
+                pltpu.VMEM((halves, ns * cap2, CHUNK), BF16),
+                pltpu.VMEM((mesh // 8, 8 * fan), jnp.int32),
+                pltpu.VMEM((mesh // 8, 8 * fan), jnp.int32),
+                pltpu.VMEM((heads, mesh, 128), BF16),
                 pltpu.VMEM((ns * cap2, width), F32),
                 pltpu.VMEM((ns, cap2, width), F32),
+                pltpu.VMEM((ns * cap2, mesh), F32),
                 pltpu.VMEM((ns * cap2, mesh), BF16),
                 pltpu.VMEM((mesh, ns * cap2), BF16),
                 pltpu.VMEM((mesh, mesh + 2 * reach), BF16),
@@ -529,7 +560,7 @@
             compiler_params=pltpu.CompilerParams(
                 collective_id=0,
                 has_side_effects=True,
-                vmem_limit_bytes=62 * 1024 * 1024,
+                vmem_limit_bytes=56 * 1024 * 1024,
             ),
             cost_estimate=pl.CostEstimate(
                 flops=12_000_000_000, bytes_accessed=10_000_000, transcendentals=0
@@ -542,13 +573,10 @@
             processor_weight,
             decoder_weight,
             g2m_send,
-            key,
-            low,
-            flat,
-            flat.reshape(ns * cap2, 1),
+            g2m_edges,
+            m2g_send.T,
             m2g_edges.T,
-            rim_t,
-            rim,
+            m2m_edges.T,
         )
     )
 

time: 137 us -> 121 us (0.88)
  Pallas kernels: 124 us -> 112 us
  other arithmetic: 3.11 us -> 0 us
  local copies, waits for them, and re-layouts: 9.75 us -> 8.25 us
    pallas_call x1, Pallas kernels: 124 us -> 112 us  [local(): pl.pallas_call(functools.partial(kernel, (ns, nc, fan, fan_m, fan_d)), ou...]
    unnamed x12, local copies, waits for them, and re-layouts: 5.24 us -> 8.25 us
    reshape x3 -> x0, local copies, waits for them, and re-layouts: 2.92 us -> none  [the longest x1 1.44 us: local(): flat = m2g_send.reshape(1, ns * cap2)]
    add x3 -> x0, other arithmetic: 2.11 us -> none  [local(): rim_t = (m2m_edges.T - me * mesh - rows + reach) % (ns * mesh) + rows]
where the time goes in v2:
time: 121 us; the launch traced here: 120 us
  Pallas kernels  112 us (93%)
  local copies, waits for them, and re-layouts  8.25 us (7%)
    pallas_call x1, Pallas kernels, local(): pl.pallas_call(functools.partial(kernel, (ns, nc, fan, fan_m, fan_d)), ou...  112 us
    unnamed x12, local copies, waits for them, and re-layouts  8.25 us

profile of v2, /device:TPU:1, one launch (start us, length us, event | category | flops | bytes accessed | tf_op | source)
XLA Modules:
  0.0 120.5 jit_solution(1246824095685108872)
XLA Ops:
  0.6 1.4 %copy.14 = s32[32,40]{0,1:T(8,128)} copy(s32[32,40]{1,0:T(8,128)} %param.17) | data formatting | bytes 10240 | tf_op args[7]
  2.0 1.6 %copy.15.source_ref = s32[320,40]{1,0:T(8,128)} copy(s32[320,40]{0,1:T(8,128)} %param.16) | data formatting | bytes 102400 | tf_op args[6]
  3.6 111.6 %encode_process_decode.1 = (bf16[8192,128]{1,0:T(8,128)(2,1)}, f32[512,128]{1,0:T(8,128)}, f32[512,128]{1,0:T(8,128)}, f32[512,128]{1,0:T(8,128)}) custom-call(bf16[8192,128]{1,0:T(8,128)(2,1)} %grid_ref.1, bf16[8192,128]{1,0:T(8,128)(2,1)} %cot_ref.1, bf16[512,128]{1,0:T(8,128)(2,1)} %we_ref.1, bf16[512,128]{1,0:T(8,128)(2,1)} %wp_ref.1, ...), custom_call_target="tpu_custom_call" | custom-call | flops 12000000000 | bytes 10000000 | tf_op jit(solution)/shard_map/encode_process_decode/pallas_call | solution.py:504
  115.2 0.0 copy-start.2
  115.2 0.0 copy-start.1
  115.2 0.0 copy-start
  115.2 3.1 %copy.20 = bf16[8192,128]{1,0:T(8,128)(2,1)} copy(bf16[8192,128]{1,0:T(8,128)(2,1)} %get-tuple-element.8) | data formatting | bytes 4194304
  118.4 0.0 copy-done.2
  118.4 0.7 copy.21
  119.1 0.0 copy-done.1
  119.1 0.7 copy.22
  119.8 0.0 copy-done
  119.8 0.7 copy.23
Async XLA Ops:
  115.2 3.1 %copy-start.2 = (f32[512,128]{1,0:T(8,128)S(1)}, f32[512,128]{1,0:T(8,128)}, u32[]{:S(2)}) copy-start(f32[512,128]{1,0:T(8,128)} %get-tuple-element.9) | copy-start | bytes 786436
  115.2 3.8 %copy-start.1 = (f32[512,128]{1,0:T(8,128)S(1)}, f32[512,128]{1,0:T(8,128)}, u32[]{:S(2)}) copy-start(f32[512,128]{1,0:T(8,128)} %get-tuple-element.10) | copy-start | bytes 786436
  115.2 4.5 %copy-start = (f32[512,128]{1,0:T(8,128)S(1)}, f32[512,128]{1,0:T(8,128)}, u32[]{:S(2)}) copy-start(f32[512,128]{1,0:T(8,128)} %get-tuple-element.11) | copy-start | bytes 786436

commit v3 on v2

--- a/solution.py
+++ b/solution.py
@@ -65,10 +65,12 @@
     recv,
     at_even,
     at_odd,
+    senders,
     key,
     low,
     counts,
     slot_grad,
+    back_out,
     back,
     sel32,
     sel,
@@ -85,7 +87,6 @@
     first,
     first_full,
     ext,
-    neighbour,
     mid_full,
     out_rows,
     slots,
@@ -108,11 +109,10 @@
     me = lax.axis_index("space")
     my = lax.axis_index("chan")
     grid_rows, width = grid_ref.shape
-    cap = send_ref.shape[1]
+    cap = recv.shape[1]
     mesh = state_sum.shape[0]
-    cap2 = back.shape[1]
-    heads = counts.shape[0]
-    per = cap // 128
+    cap2 = mesh_send_ref.shape[1]
+    pad2 = back.shape[1]
     reach = halo_low.shape[0]
     share = grads_b.shape[1]
     fan_scale = fan ** (-0.5)
@@ -175,15 +175,21 @@
     lax.fori_loop(0, grid_rows // CHUNK, widen, 0)
     pl.semaphore_wait(barrier, ns + nc - 2)
 
+    lanes = 8 if ns % 8 == 0 else ns
+
     def pick(peer):
-        def some(i, carry):
-            base = pl.multiple_of(i * 32, 32)
-            rows = [grid32[pl.ds(send_ref[peer, base + u], 1), :] for u in range(32)]
-            for u in range(32):
-                stage[pl.ds(base + u, 1), :] = rows[u]
-            return carry
-
-        lax.fori_loop(0, cap // 32, some, 0)
+        first_of = (peer // lanes) * (lanes * cap) + lax.rem(peer, lanes) * 128
+        for part in range(cap // 128):
+
+            def some(i, carry):
+                base = pl.multiple_of(i * 64, 64)
+                at = first_of + part * (lanes * 128) + base
+                rows = [grid32[pl.ds(send_ref[at + u], 1), :] for u in range(64)]
+                for u in range(64):
+                    stage[pl.ds(part * 128 + base + u, 1), :] = rows[u]
+                return carry
+
+            lax.fori_loop(0, 2, some, 0)
 
     def pick_and_send(peer):
         pick(peer)
@@ -234,40 +240,43 @@
         spread(at_even, last, 2 * last, lo, hi)
         build(at_odd, last, 2 * last + 1, lo, hi)
     spread(at_odd, last, 2 * last + 1, 0, all_slots)
-    slot_grad[...] = slot_grad[...] * fan_d_scale
-    own_rows = pl.ds(pl.multiple_of(me * cap2, cap2), cap2)
+    back_out[:, 0:cap2, :] = (
+        (slot_grad[...] * fan_d_scale).reshape(ns, cap2, width).astype(BF16)
+    )
+    back_out[:, cap2:pad2, :] = jnp.zeros((ns, pad2 - cap2, width), BF16)
 
     def send_back(peer):
-        rows = pl.ds(pl.multiple_of(peer * cap2, cap2), cap2)
-        remote(slot_grad.at[rows], back.at[me], 1, peer, my).start()
+        remote(back_out.at[peer], back.at[me], 1, peer, my).start()
 
     peers(send_back)
-    back[me] = slot_grad[own_rows, :]
+    back[me] = back_out[me]
 
     octets = mesh // 8
-    parts = [source_ref[pl.ds(u, octets, stride=8), :] for u in range(8)]
-    key[...] = jnp.concatenate([(part // 128) * 8 + u for u, part in enumerate(parts)], axis=1)
-    low[...] = jnp.concatenate([part % 128 for part in parts], axis=1)
+    senders[...] = source_ref[...].astype(F32).T
+    parts = [
+        senders[pl.ds(u, octets, stride=8), :].astype(jnp.int32) for u in range(8)
+    ]
+    key[...] = jnp.concatenate([(part // cap) * 8 + u for u, part in enumerate(parts)], axis=1)
+    low[...] = jnp.concatenate([part % cap for part in parts], axis=1)
     big = row_iota(128, key.shape[1])
+
+    def one_hot(row, rows):
+        step = min(rows, 128)
+        return jnp.concatenate(
+            [ones_where(big[0:step] == narrow(row, base)) for base in range(0, rows, step)], axis=0
+        )
 
     def count_step(g, carry):
         found = []
         for u in range(2):
-            top = key[pl.ds(2 * g + u, 1), :]
-            right = ones_where(big == narrow(low[pl.ds(2 * g + u, 1), :], 0))
-            found.append(
-                [
-                    dot_nt(ones_where(big == narrow(top, kb * 128)), right).reshape(16, 8, 128)
-                    for kb in range(heads * 8 // 128)
-                ]
-            )
+            row = pl.ds(2 * g + u, 1)
+            left = one_hot(key[row, :], 8 * ns)
+            found.append(dot_nt(left, one_hot(low[row, :], cap)).reshape(ns, 8, cap))
         rows = pl.ds(pl.multiple_of(g * 16, 16), 16)
-        for kb in range(heads * 8 // 128):
-            pair = jnp.concatenate([found[0][kb], found[1][kb]], axis=1)
-            counts[kb * 16 : (kb + 1) * 16, rows, :] = pair.astype(BF16)
+        counts[:, rows, :] = jnp.concatenate(found, axis=1).astype(BF16)
         return carry
 
-    lax.fori_loop(0, mesh // 16, count_step, 0, unroll=2)
+    lax.fori_loop(0, mesh // 16, count_step, 0, unroll=5 if mesh % 80 == 0 else 1)
 
     node = lax.broadcasted_iota(jnp.int32, near_ref.shape, 1)
     span = ns * mesh
@@ -280,49 +289,51 @@
         total = total + jnp.where(rows_iota == offset[j : j + 1, :], 1.0, 0.0)
     rimt[...] = total.astype(BF16)
     rim[...] = total.T.astype(BF16)
-    lane_iota = lax.broadcasted_iota(jnp.int32, (cap2, mesh), 1)
+    mesh_send = mesh_send_ref[...].astype(F32).T
+    lane_iota = lax.broadcasted_iota(jnp.int32, (cap2, mesh), 1).astype(F32)
     for p in range(ns):
-        column = mesh_send_ref[:, p : p + 1]
-        sel32[p * cap2 : (p + 1) * cap2, :] = jnp.where(lane_iota == column, 1.0, 0.0)
+        hot = jnp.where(lane_iota == mesh_send[:, p : p + 1], 1.0, 0.0)
+        sel32[p * pad2 : p * pad2 + cap2, :] = hot
+        sel32[p * pad2 + cap2 : (p + 1) * pad2, :] = jnp.zeros((pad2 - cap2, mesh), F32)
     sel[...] = sel32[...].astype(BF16)
     selt[...] = sel32[...].T.astype(BF16)
 
+    quad = 4
+    quads = ns // quad
+
+    def absorb(first_source):
+        total = dot(counts[first_source], recv[first_source])
+        for u in range(1, quad):
+            total = total + dot(counts[first_source + u], recv[first_source + u])
+        return total
+
+    def arrived(source):
+        remote(recv.at[source], recv.at[source], 0, me, my, gsem.at[source]).wait_recv()
+
+    state_sum[...] = jnp.zeros(state_sum.shape, F32)
+
+    def absorb_step(k, carry):
+        base = lax.rem(me // quad + quads - k, quads) * quad
+        for u in range(quad):
+            arrived(base + u)
+        state_sum[...] += absorb(base)
+        return carry
+
+    lax.fori_loop(1, quads, absorb_step, 0)
+    own = (me // quad) * quad
+    for u in range(1, quad):
+        arrived(own + lax.rem(me + u, quad))
+    state_full[my] = (state_sum[...] + absorb(own)).astype(BF16)
+
+    def send_state(c):
+        remote(state_full.at[my], state_full.at[my], 3, me, c).start()
+
+    chans(send_state)
+
     wait_space(back, 1)
-    dgrad[...] = dot(selt[...], back[...].reshape(all_slots, width).astype(BF16)).astype(BF16)
+    dgrad[...] = dot(selt[...], back[...].reshape(ns * pad2, width)).astype(BF16)
     for c in range(nc):
         second_part[c] = dot_nt(dgrad[...], wd_ref[c * width : (c + 1) * width, :]).astype(BF16)
-
-    def send_second(c):
-        remote(second_part.at[c], second_recv.at[my], 2, me, c).start()
-
-    chans(send_second)
-    second_recv[my] = second_part[my]
-
-    def absorb(source):
-        left = jnp.concatenate([counts[source * per + h] for h in range(per)], axis=1)
-        return dot(left, recv[source])
-
-    state_sum[...] = absorb(me)
-
-    def absorb_step(k, carry):
-        source = lax.rem(me + ns - k, ns)
-        remote(recv.at[source], recv.at[source], 0, me, my, gsem.at[source]).wait_recv()
-        state_sum[...] += absorb(source)
-        return carry
-
-    lax.fori_loop(1, ns, absorb_step, 0)
-    state_full[my] = state_sum[...].astype(BF16)
-
-    def send_state(c):
-        remote(state_full.at[my], state_full.at[my], 3, me, c).start()
-
-    chans(send_state)
-
-    wait_chan(second_recv, 2)
-    total = second_recv[0].astype(F32)
-    for c in range(1, nc):
-        total = total + second_recv[c].astype(F32)
-    second[...] = total
 
     wait_chan(state_full, 3)
     total = dot(state_full[0], we_ref[0:width, :])
@@ -336,49 +347,47 @@
         remote(first_full.at[my], first_full.at[my], 4, me, c).start()
 
     chans(send_first)
+
+    def send_second(c):
+        remote(second_part.at[c], second_recv.at[my], 2, me, c).start()
+
+    chans(send_second)
+    second_recv[my] = second_part[my]
     first[...] = first_full[my].astype(F32)
+    gathered[...] = slope(gathered[...]) * fan_scale
     wait_chan(first_full, 4)
     total = dot(first_full[0], wp_ref[0:width, :])
     for c in range(1, nc):
         total = total + dot(first_full[c], wp_ref[c * width : (c + 1) * width, :])
     ext[reach : reach + mesh, :] = total.astype(BF16)
-    to_next = remote(
-        ext.at[pl.ds(mesh, reach)], ext.at[pl.ds(0, reach)], 5, nxt, my
-    )
+    to_next = remote(ext.at[pl.ds(mesh, reach)], ext.at[pl.ds(0, reach)], 5, nxt, my)
     to_prev = remote(
         ext.at[pl.ds(reach, reach)], ext.at[pl.ds(reach + mesh, reach)], 6, prv, my
     )
     to_next.start()
     to_prev.start()
+    wait_chan(second_recv, 2)
+    total = second_recv[0].astype(F32)
+    for c in range(1, nc):
+        total = total + second_recv[c].astype(F32)
+    second[...] = total
     to_next.wait()
     to_prev.wait()
     total = dot(rim[...], ext[...]) * fan_m_scale
-    neighbour[...] = total
-    mid_full[my] = (first[...] + total * jax.nn.sigmoid(total)).astype(BF16)
+    sigmoid = jax.nn.sigmoid(total)
+    mid_full[my] = (first[...] + total * sigmoid).astype(BF16)
 
     def send_mid(c):
         remote(mid_full.at[my], mid_full.at[my], 7, me, c).start()
 
     chans(send_mid)
-    pre = (second[...] * slope(neighbour[...]) * fan_m_scale).astype(BF16)
+    slant = sigmoid * (1.0 + total * (1.0 - sigmoid))
+    pre = (second[...] * slant * fan_m_scale).astype(BF16)
     rim_grad[...] = dot(rimt[...], pre)
     down = remote(rim_grad.at[pl.ds(0, reach)], halo_high, 8, prv, my)
     up = remote(rim_grad.at[pl.ds(reach + mesh, reach)], halo_low, 9, nxt, my)
     down.start()
     up.start()
-
-    wait_chan(mid_full, 7)
-    total = dot(mid_full[0], wd_ref[0:width, :])
-    for c in range(1, nc):
-        total = total + dot(mid_full[c], wd_ref[c * width : (c + 1) * width, :])
-    out_rows[...] = dot(sel[...], total.astype(BF16)).reshape(out_rows.shape)
-
-    def send_rows(peer):
-        remote(out_rows.at[peer], slots.at[me], 10, peer, my).start()
-
-    peers(send_rows)
-    slots[me] = out_rows[me]
-
     down.wait()
     up.wait()
     rim_grad[reach : 2 * reach, :] += halo_low[...]
@@ -392,41 +401,47 @@
 
     chans(send_proj)
     proj_recv[my] = proj_part[my]
+
+    wait_chan(mid_full, 7)
+    total = dot(mid_full[0], wd_ref[0:width, :])
+    for c in range(1, nc):
+        total = total + dot(mid_full[c], wd_ref[c * width : (c + 1) * width, :])
+    out_rows[...] = dot(sel[...], total.astype(BF16)).astype(BF16).reshape(out_rows.shape)
+
+    def send_rows(peer):
+        remote(out_rows.at[peer], slots.at[me], 10, peer, my).start()
+
+    peers(send_rows)
+    slots[me] = out_rows[me]
     blocks = width // share
+
+    def split(grad):
+        return grad.astype(BF16).reshape(blocks, share, width)
+
     for c in range(nc):
         cut = slice(c * blocks, (c + 1) * blocks)
-        grads_a[cut, 0:share, :] = (
-            dot_tn(mid_full[c], dgrad[...]).astype(BF16).reshape(blocks, share, width)
-        )
-        grads_a[cut, share : 2 * share, :] = (
-            dot_tn(first_full[c], projected).astype(BF16).reshape(blocks, share, width)
-        )
-
-    def send_a(peer):
-        remote(grads_a.at[peer], grecv_a.at[me], 12, peer, my).start()
-
-    peers(send_a)
-    grecv_a[me] = grads_a[me]
+        grads_a[cut, 0:share, :] = split(dot_tn(mid_full[c], dgrad[...]))
+        grads_a[cut, share : 2 * share, :] = split(dot_tn(first_full[c], projected))
 
     wait_chan(proj_recv, 11)
     total = second[...]
     for c in range(nc):
         total = total + proj_recv[c].astype(F32)
-    sum_grad = (total * slope(gathered[...]) * fan_scale).astype(BF16)
+    sum_grad = (total * gathered[...]).astype(BF16)
     for c in range(nc):
-        cut = slice(c * blocks, (c + 1) * blocks)
-        grads_b[cut] = (
-            dot_tn(state_full[c], sum_grad).astype(BF16).reshape(blocks, share, width)
-        )
-
-    def send_b(peer):
+        grads_b[c * blocks : (c + 1) * blocks] = split(dot_tn(state_full[c], sum_grad))
+
+    def send_grads(peer):
         remote(grads_b.at[peer], grecv_b.at[me], 13, peer, my).start()
-
-    peers(send_b)
+        remote(grads_a.at[peer], grecv_a.at[me], 12, peer, my).start()
+
+    peers(send_grads)
+    grecv_a[me] = grads_a[me]
     grecv_b[me] = grads_b[me]
 
     wait_space(slots, 10)
-    slots_t[...] = slots[...].reshape(all_slots, width).T.astype(BF16)
+    rows = slots[...].astype(F32)[:, 0:cap2, :].reshape(all_slots, width)
+    slots_t[...] = rows.T.astype(BF16)
 
     def predict(t, carry):
         for u, buf in enumerate((at_even, at_odd)):
@@ -494,7 +509,9 @@
     reach = min(REACH, mesh // 2)
     full = encoder_weight.shape[0]
     share = full // ns
-    heads = ns * cap // 128
+    pad2 = (cap2 + 15) // 16 * 16
+    tall = 8 if ns % 8 == 0 else ns
+    send = g2m_send.reshape(ns // tall, tall, cap // 128, 128).transpose(0, 2, 1, 3).reshape(-1)
     halves = grid_rows // CHUNK // 2
 
     vmem = pl.BlockSpec(memory_space=pltpu.VMEM)
@@ -518,14 +535,16 @@
                 pltpu.VMEM((ns, cap, width), BF16),
                 pltpu.VMEM((halves, ns * cap2, CHUNK), BF16),
                 pltpu.VMEM((halves, ns * cap2, CHUNK), BF16),
+                pltpu.VMEM((mesh, fan), F32),
                 pltpu.VMEM((mesh // 8, 8 * fan), jnp.int32),
                 pltpu.VMEM((mesh // 8, 8 * fan), jnp.int32),
-                pltpu.VMEM((heads, mesh, 128), BF16),
+                pltpu.VMEM((ns, mesh, cap), BF16),
                 pltpu.VMEM((ns * cap2, width), F32),
-                pltpu.VMEM((ns, cap2, width), F32),
-                pltpu.VMEM((ns * cap2, mesh), F32),
-                pltpu.VMEM((ns * cap2, mesh), BF16),
-                pltpu.VMEM((mesh, ns * cap2), BF16),
+                pltpu.VMEM((ns, pad2, width), BF16),
+                pltpu.VMEM((ns, pad2, width), BF16),
+                pltpu.VMEM((ns * pad2, mesh), F32),
+                pltpu.VMEM((ns * pad2, mesh), BF16),
+                pltpu.VMEM((mesh, ns * pad2), BF16),
                 pltpu.VMEM((mesh, mesh + 2 * reach), BF16),
                 pltpu.VMEM((mesh + 2 * reach, mesh), BF16),
                 pltpu.VMEM((mesh, width), BF16),
@@ -538,10 +557,9 @@
                 pltpu.VMEM((mesh, width), F32),
                 pltpu.VMEM((nc, mesh, width), BF16),
                 pltpu.VMEM((mesh + 2 * reach, width), BF16),
-                pltpu.VMEM((mesh, width), F32),
                 pltpu.VMEM((nc, mesh, width), BF16),
-                pltpu.VMEM((ns, cap2, width), F32),
-                pltpu.VMEM((ns, cap2, width), F32),
+                pltpu.VMEM((ns, pad2, width), BF16),
+                pltpu.VMEM((ns, pad2, width), BF16),
                 pltpu.VMEM((width, ns * cap2), BF16),
                 pltpu.VMEM((mesh + 2 * reach, width), F32),
                 pltpu.VMEM((reach, width), F32),
@@ -572,9 +590,9 @@
             encoder_weight,
             processor_weight,
             decoder_weight,
-            g2m_send,
-            g2m_edges,
-            m2g_send.T,
+            send,
+            g2m_edges.T,
+            m2g_send,
             m2g_edges.T,
             m2m_edges.T,
         )

time: 121 us -> 100 us (0.83)
  Pallas kernels: 112 us -> 94.4 us
  local copies, waits for them, and re-layouts: 8.25 us -> 5.23 us
    pallas_call x1, Pallas kernels: 112 us -> 94.4 us  [local(): pl.pallas_call(functools.partial(kernel, (ns, nc, fan, fan_m, fan_d)), ou...]
    unnamed x12 -> x10, local copies, waits for them, and re-layouts: 8.25 us -> 5.23 us
where the time goes in v3:
time: 100 us
  Pallas kernels  94.4 us (94%)
  local copies, waits for them, and re-layouts  5.23 us (5%)
    pallas_call x1, Pallas kernels, local(): pl.pallas_call(functools.partial(kernel, (ns, nc, fan, fan_m, fan_d)), ou...  94.4 us
    unnamed x10, local copies, waits for them, and re-layouts  5.23 us

profile of v3, /device:TPU:1, one launch (start us, length us, event | category | flops | bytes accessed | tf_op | source)
XLA Modules:
  0.0 100.3 jit_solution(1726071444575328699)
XLA Ops:
  0.6 94.4 %encode_process_decode.1 = (bf16[8192,128]{1,0:T(8,128)(2,1)}, f32[512,128]{1,0:T(8,128)}, f32[512,128]{1,0:T(8,128)}, f32[512,128]{1,0:T(8,128)}) custom-call(bf16[8192,128]{1,0:T(8,128)(2,1)} %grid_ref.1, bf16[8192,128]{1,0:T(8,128)(2,1)} %cot_ref.1, bf16[512,128]{1,0:T(8,128)(2,1)} %we_ref.1, bf16[512,128]{1,0:T(8,128)(2,1)} %wp_ref.1, ...), custom_call_target="tpu_custom_call" | custom-call | flops 12000000000 | bytes 10000000 | tf_op jit(solution)/shard_map/encode_process_decode/pallas_call | solution.py:521
  95.0 0.0 copy-start.2
  95.0 0.0 copy-start.1
  95.0 0.0 copy-start
  95.0 3.1 %copy.18 = bf16[8192,128]{1,0:T(8,128)(2,1)} copy(bf16[8192,128]{1,0:T(8,128)(2,1)} %get-tuple-element.8) | data formatting | bytes 4194304
  98.1 0.0 copy-done.2
  98.2 0.7 copy.19
  98.9 0.0 copy-done.1
  98.9 0.7 copy.20
  99.6 0.0 copy-done
  99.6 0.7 copy.21
Async XLA Ops:
  95.0 3.1 %copy-start.2 = (f32[512,128]{1,0:T(8,128)S(1)}, f32[512,128]{1,0:T(8,128)}, u32[]{:S(2)}) copy-start(f32[512,128]{1,0:T(8,128)} %get-tuple-element.9) | copy-start | bytes 786436
  95.0 3.8 %copy-start.1 = (f32[512,128]{1,0:T(8,128)S(1)}, f32[512,128]{1,0:T(8,128)}, u32[]{:S(2)}) copy-start(f32[512,128]{1,0:T(8,128)} %get-tuple-element.10) | copy-start | bytes 786436
  95.0 4.5 %copy-start = (f32[512,128]{1,0:T(8,128)S(1)}, f32[512,128]{1,0:T(8,128)}, u32[]{:S(2)}) copy-start(f32[512,128]{1,0:T(8,128)} %get-tuple-element.11) | copy-start | bytes 786436

commit v4 on v3

--- a/solution.py
+++ b/solution.py
@@ -45,11 +45,11 @@
 
 def kernel(
     sizes,
-    grid_ref,
-    cot_ref,
-    we_ref,
-    wp_ref,
-    wd_ref,
+    grid_hbm,
+    cot_hbm,
+    we_hbm,
+    wp_hbm,
+    wd_hbm,
     send_ref,
     source_ref,
     mesh_send_ref,
@@ -59,6 +59,11 @@
     ge_ref,
     gp_ref,
     gd_ref,
+    grid_ref,
+    cot_ref,
+    we_all,
+    wp_all,
+    wd_ref,
     grid32,
     stage,
     sendbuf,
@@ -83,9 +88,10 @@
     second,
     state_sum,
     state_full,
+    state_rows,
     gathered,
-    first,
-    first_full,
+    first_rows,
+    proj_rows,
     ext,
     mid_full,
     out_rows,
@@ -100,10 +106,12 @@
     grads_b,
     grecv_a,
     grecv_b,
-    gout,
+    gout_a,
+    gout_b,
     ssem,
     rsem,
     gsem,
+    isem,
 ):
     ns, nc, fan, fan_m, fan_d = sizes
     me = lax.axis_index("space")
@@ -132,12 +140,21 @@
             device_id_type=MESH,
         )
 
-    def peers(body):
+    side = 4 if ns == 32 else 1
+
+    def at_distance(k, sign):
+        if side == 1:
+            return lax.rem(me + ns + sign * k, ns)
+        along_x = lax.rem(me // 8 + side + sign * lax.rem(k, side), side)
+        along_y = lax.rem(me // 2 + side + sign * lax.rem(k // side, side), side)
+        return along_x * 8 + along_y * 2 + lax.rem(me + k // 16, 2)
+
+    def peers(body, lo=1, hi=ns):
         def step(k, carry):
-            body(lax.rem(me + k, ns))
+            body(at_distance(k, 1))
             return carry
 
-        lax.fori_loop(1, ns, step, 0)
+        lax.fori_loop(lo, hi, step, 0)
 
     def chans(body):
         for k in range(1, nc):
@@ -155,6 +172,19 @@
         part = buf.at[pl.ds(0, count)]
         remote(part, part, which, me, my).wait_send()
 
+    loads = [
+        pltpu.make_async_copy(src, dst, isem.at[i])
+        for i, (src, dst) in enumerate(
+            (
+                (grid_hbm, grid_ref),
+                (cot_hbm, cot_ref),
+                (we_hbm, we_all.at[my]),
+                (wp_hbm, wp_all.at[my]),
+                (wd_hbm, wd_ref),
+            )
+        )
+    ]
+    loads[0].start()
     barrier = pltpu.get_barrier_semaphore()
 
     def greet(peer):
@@ -166,6 +196,16 @@
         pl.semaphore_signal(barrier, inc=1, device_id=(me, c), device_id_type=MESH)
 
     chans(greet_chan)
+
+    def greet_beside(c):
+        for space in (nxt, prv):
+            pl.semaphore_signal(barrier, inc=1, device_id=(space, c), device_id_type=MESH)
+
+    chans(greet_beside)
+
+    for load in loads[1:]:
+        load.start()
+    loads[0].wait()
 
     def widen(i, carry):
         rows = pl.ds(pl.multiple_of(i * CHUNK, CHUNK), CHUNK)
@@ -173,7 +213,6 @@
         return carry
 
     lax.fori_loop(0, grid_rows // CHUNK, widen, 0)
-    pl.semaphore_wait(barrier, ns + nc - 2)
 
     lanes = 8 if ns % 8 == 0 else ns
 
@@ -191,14 +230,40 @@
 
             lax.fori_loop(0, 2, some, 0)
 
-    def pick_and_send(peer):
+    def pick_for(peer):
         pick(peer)
         sendbuf[peer] = stage[...].astype(BF16)
+
+    def send_picked(peer):
         remote(sendbuf.at[peer], recv.at[me], 0, peer, my, gsem.at[me]).start()
 
-    peers(pick_and_send)
-    pick(me)
-    recv[me] = stage[...].astype(BF16)
+    def pick_and_send(peer):
+        pick_for(peer)
+        send_picked(peer)
+
+    early = ns // 2
+    peers(pick_for, 1, early)
+
+    mesh_send = mesh_send_ref[...].astype(F32).T
+    lane_iota = lax.broadcasted_iota(jnp.int32, (cap2, mesh), 1).astype(F32)
+    for p in range(ns):
+        hot = jnp.where(lane_iota == mesh_send[:, p : p + 1], 1.0, 0.0)
+        sel32[p * pad2 : p * pad2 + cap2, :] = hot
+        if pad2 > cap2:
+            sel32[p * pad2 + cap2 : (p + 1) * pad2, :] = jnp.zeros((pad2 - cap2, mesh), F32)
+    sel[...] = sel32[...].astype(BF16)
+    selt[...] = sel32[...].T.astype(BF16)
+
+    pl.semaphore_wait(barrier, ns - 1 + 3 * (nc - 1))
+    peers(send_picked, 1, early)
+    for load in loads[1:]:
+        load.wait()
+
+    def send_weights(c):
+        remote(we_all.at[my], we_all.at[my], 16, me, c).start()
+        remote(wp_all.at[my], wp_all.at[my], 17, me, c).start()
+
+    chans(send_weights)
 
     iota = row_iota(128, 128)
     slot_grad[...] = jnp.zeros(slot_grad.shape, F32)
@@ -243,13 +308,18 @@
     back_out[:, 0:cap2, :] = (
         (slot_grad[...] * fan_d_scale).reshape(ns, cap2, width).astype(BF16)
     )
-    back_out[:, cap2:pad2, :] = jnp.zeros((ns, pad2 - cap2, width), BF16)
+    if pad2 > cap2:
+        back_out[:, cap2:pad2, :] = jnp.zeros((ns, pad2 - cap2, width), BF16)
 
     def send_back(peer):
         remote(back_out.at[peer], back.at[me], 1, peer, my).start()
 
     peers(send_back)
     back[me] = back_out[me]
+
+    peers(pick_and_send, early, ns)
+    pick(me)
+    recv[me] = stage[...].astype(BF16)
 
     octets = mesh // 8
     senders[...] = source_ref[...].astype(F32).T
@@ -277,6 +347,50 @@
         return carry
 
     lax.fori_loop(0, mesh // 16, count_step, 0, unroll=5 if mesh % 80 == 0 else 1)
+
+    wait_space(back, 1)
+    dgrad[...] = dot(selt[...], back[...].reshape(ns * pad2, width)).astype(BF16)
+    for c in range(nc):
+        second_part[c] = dot_nt(dgrad[...], wd_ref[c * width : (c + 1) * width, :]).astype(BF16)
+
+    def send_second(c):
+        remote(second_part.at[c], second_recv.at[my], 2, me, c).start()
+
+    chans(send_second)
+    second_recv[my] = second_part[my]
+    def absorb(k, waits):
+        total = None
+        for u in range(4):
+            source = at_distance(4 * k + u, -1)
+            if waits or u > 0:
+                remote(recv.at[source], recv.at[source], 0, me, my, gsem.at[source]).wait_recv()
+            term = dot(counts[source], recv[source])
+            total = term if total is None else total + term
+        return total
+
+    state_sum[...] = absorb(0, False)
+
+    def absorb_step(k, carry):
+        state_sum[...] += absorb(k, True)
+        return carry
+
+    lax.fori_loop(1, ns // 4, absorb_step, 0)
+    state_full[my] = state_sum[...].astype(BF16)
+
+    piece = mesh // nc
+    own_piece = pl.ds(pl.multiple_of(my * piece, 16), piece)
+
+    def send_rows_of_sum(c):
+        rows = pl.ds(pl.multiple_of(c * piece, 16), piece)
+        remote(state_full.at[my, rows], state_rows.at[my], 18, me, c).start()
+
+    chans(send_rows_of_sum)
+    state_rows[my] = state_full[my, own_piece, :]
+
+    def send_state(c):
+        remote(state_full.at[my], state_full.at[my], 3, me, c).start()
+
+    chans(send_state)
 
     node = lax.broadcasted_iota(jnp.int32, near_ref.shape, 1)
     span = ns * mesh
@@ -289,98 +403,54 @@
         total = total + jnp.where(rows_iota == offset[j : j + 1, :], 1.0, 0.0)
     rimt[...] = total.astype(BF16)
     rim[...] = total.T.astype(BF16)
-    mesh_send = mesh_send_ref[...].astype(F32).T
-    lane_iota = lax.broadcasted_iota(jnp.int32, (cap2, mesh), 1).astype(F32)
-    for p in range(ns):
-        hot = jnp.where(lane_iota == mesh_send[:, p : p + 1], 1.0, 0.0)
-        sel32[p * pad2 : p * pad2 + cap2, :] = hot
-        sel32[p * pad2 + cap2 : (p + 1) * pad2, :] = jnp.zeros((pad2 - cap2, mesh), F32)
-    sel[...] = sel32[...].astype(BF16)
-    selt[...] = sel32[...].T.astype(BF16)
-
-    quad = 4
-    quads = ns // quad
-
-    def absorb(first_source):
-        total = dot(counts[first_source], recv[first_source])
-        for u in range(1, quad):
-            total = total + dot(counts[first_source + u], recv[first_source + u])
-        return total
-
-    def arrived(source):
-        remote(recv.at[source], recv.at[source], 0, me, my, gsem.at[source]).wait_recv()
-
-    state_sum[...] = jnp.zeros(state_sum.shape, F32)
-
-    def absorb_step(k, carry):
-        base = lax.rem(me // quad + quads - k, quads) * quad
-        for u in range(quad):
-            arrived(base + u)
-        state_sum[...] += absorb(base)
-        return carry
-
-    lax.fori_loop(1, quads, absorb_step, 0)
-    own = (me // quad) * quad
-    for u in range(1, quad):
-        arrived(own + lax.rem(me + u, quad))
-    state_full[my] = (state_sum[...] + absorb(own)).astype(BF16)
-
-    def send_state(c):
-        remote(state_full.at[my], state_full.at[my], 3, me, c).start()
-
-    chans(send_state)
-
-    wait_space(back, 1)
-    dgrad[...] = dot(selt[...], back[...].reshape(ns * pad2, width)).astype(BF16)
+    wait_chan(we_all, 16)
+    wait_chan(wp_all, 17)
+    wait_chan(state_rows, 18)
+    whole = jnp.concatenate([state_rows[c] for c in range(nc)], axis=1)
+    total = jnp.concatenate([dot(whole, we_all[c]) for c in range(nc)], axis=1) * fan_scale
+    latent = (total * jax.nn.sigmoid(total)).astype(BF16)
+    first_rows[my] = latent
     for c in range(nc):
-        second_part[c] = dot_nt(dgrad[...], wd_ref[c * width : (c + 1) * width, :]).astype(BF16)
-
-    wait_chan(state_full, 3)
-    total = dot(state_full[0], we_ref[0:width, :])
-    for c in range(1, nc):
-        total = total + dot(state_full[c], we_ref[c * width : (c + 1) * width, :])
-    total = total * fan_scale
-    gathered[...] = total
-    first_full[my] = (total * jax.nn.sigmoid(total)).astype(BF16)
+        proj_rows[c] = dot(latent, wp_all[c]).astype(BF16)
+    upper = my >= nc // 2
+    beside = jnp.where(upper, nxt, prv)
+    inner = pl.ds(pl.multiple_of(reach + my * piece, 16), piece)
+    outer = pl.ds(
+        pl.multiple_of(jnp.where(upper, my * piece - (mesh - reach), reach + mesh + my * piece), 16),
+        piece,
+    )
+
+    def send_projected(c):
+        remote(proj_rows.at[c], ext.at[inner], 19, me, c).start()
+
+    def send_beside(c):
+        remote(proj_rows.at[c], ext.at[outer], 19, beside, c).start()
+
+    chans(send_projected)
+    send_beside(my)
+    chans(send_beside)
+    ext[inner, :] = proj_rows[my]
 
     def send_first(c):
-        remote(first_full.at[my], first_full.at[my], 4, me, c).start()
+        remote(first_rows.at[my], first_rows.at[my], 4, me, c).start()
 
     chans(send_first)
 
-    def send_second(c):
-        remote(second_part.at[c], second_recv.at[my], 2, me, c).start()
-
-    chans(send_second)
-    second_recv[my] = second_part[my]
-    first[...] = first_full[my].astype(F32)
-    gathered[...] = slope(gathered[...]) * fan_scale
-    wait_chan(first_full, 4)
-    total = dot(first_full[0], wp_ref[0:width, :])
-    for c in range(1, nc):
-        total = total + dot(first_full[c], wp_ref[c * width : (c + 1) * width, :])
-    ext[reach : reach + mesh, :] = total.astype(BF16)
-    to_next = remote(ext.at[pl.ds(mesh, reach)], ext.at[pl.ds(0, reach)], 5, nxt, my)
-    to_prev = remote(
-        ext.at[pl.ds(reach, reach)], ext.at[pl.ds(reach + mesh, reach)], 6, prv, my
-    )
-    to_next.start()
-    to_prev.start()
     wait_chan(second_recv, 2)
     total = second_recv[0].astype(F32)
     for c in range(1, nc):
         total = total + second_recv[c].astype(F32)
     second[...] = total
-    to_next.wait()
-    to_prev.wait()
+    wait_chan(state_full, 3)
+    total = dot(state_full[0], we_all[my, 0:width, :])
+    for c in range(1, nc):
+        total = total + dot(state_full[c], we_all[my, c * width : (c + 1) * width, :])
+    gathered[...] = slope(total * fan_scale) * fan_scale
+    seven = ext.at[pl.ds(0, (2 * nc - 1) * piece)]
+    remote(seven, seven, 19, me, my).wait_recv()
     total = dot(rim[...], ext[...]) * fan_m_scale
     sigmoid = jax.nn.sigmoid(total)
-    mid_full[my] = (first[...] + total * sigmoid).astype(BF16)
-
-    def send_mid(c):
-        remote(mid_full.at[my], mid_full.at[my], 7, me, c).start()
-
-    chans(send_mid)
+    silu = total * sigmoid
     slant = sigmoid * (1.0 + total * (1.0 - sigmoid))
     pre = (second[...] * slant * fan_m_scale).astype(BF16)
     rim_grad[...] = dot(rimt[...], pre)
@@ -388,13 +458,22 @@
     up = remote(rim_grad.at[pl.ds(reach + mesh, reach)], halo_low, 9, nxt, my)
     down.start()
     up.start()
+    wait_chan(first_rows, 4)
+    own_lanes = pl.ds(pl.multiple_of(my * width, width), width)
+    first = first_rows[:, :, own_lanes].reshape(mesh, width).astype(F32)
+    mid_full[my] = (first + silu).astype(BF16)
+
+    def send_mid(c):
+        remote(mid_full.at[my], mid_full.at[my], 7, me, c).start()
+
+    chans(send_mid)
     down.wait()
     up.wait()
     rim_grad[reach : 2 * reach, :] += halo_low[...]
     rim_grad[mesh : mesh + reach, :] += halo_high[...]
     projected = rim_grad[reach : reach + mesh, :].astype(BF16)
     for c in range(nc):
-        proj_part[c] = dot_nt(projected, wp_ref[c * width : (c + 1) * width, :]).astype(BF16)
+        proj_part[c] = dot_nt(projected, wp_all[my, c * width : (c + 1) * width, :]).astype(BF16)
 
     def send_proj(c):
         remote(proj_part.at[c], proj_recv.at[my], 11, me, c).start()
@@ -421,8 +500,15 @@
     for c in range(nc):
         cut = slice(c * blocks, (c + 1) * blocks)
         grads_a[cut, 0:share, :] = split(dot_tn(mid_full[c], dgrad[...]))
-        grads_a[cut, share : 2 * share, :] = split(dot_tn(first_full[c], projected))
-
+        grads_a[cut, share : 2 * share, :] = split(
+            dot_tn(first_rows[:, :, c * width : (c + 1) * width].reshape(mesh, width), projected)
+        )
+
+    def send_a(peer):
+        remote(grads_a.at[peer], grecv_a.at[me], 12, peer, my).start()
+
+    peers(send_a)
+    grecv_a[me] = grads_a[me]
     wait_chan(proj_recv, 11)
     total = second[...]
     for c in range(nc):
@@ -431,12 +517,10 @@
     for c in range(nc):
         grads_b[c * blocks : (c + 1) * blocks] = split(dot_tn(state_full[c], sum_grad))
 
-    def send_grads(peer):
+    def send_b(peer):
         remote(grads_b.at[peer], grecv_b.at[me], 13, peer, my).start()
-        remote(grads_a.at[peer], grecv_a.at[me], 12, peer, my).start()
-
-    peers(send_grads)
-    grecv_a[me] = grads_a[me]
+
+    peers(send_b)
     grecv_b[me] = grads_b[me]
 
     wait_space(slots, 10)
@@ -450,40 +534,50 @@
             pred_ref[rows, :] = (grid_ref[rows, :].astype(F32) + moved.T).astype(BF16)
         return carry
 
-    lax.fori_loop(0, steps // 4, predict, 0)
-
+    def gather_sum(got, whole):
+        total = got[0].astype(F32)
+        for source in range(1, ns):
+            total = total + got[source].astype(F32)
+        whole[me] = total.astype(BF16)
+
+    def send_out_a(peer):
+        remote(gout_a.at[me], gout_a.at[me], 14, peer, my).start()
+
+    def send_out_b(peer):
+        remote(gout_b.at[me], gout_b.at[me], 15, peer, my).start()
+
+    quarter = max(steps // 8, 1)
+    lax.fori_loop(0, quarter, predict, 0)
+    wait_space(grecv_b, 13)
+    gather_sum(grecv_b, gout_b)
+    peers(send_out_b)
     wait_space(grecv_a, 12)
-    wait_space(grecv_b, 13)
-    total_a = grecv_a[0].astype(F32)
-    total_b = grecv_b[0].astype(F32)
-    for s in range(1, ns):
-        total_a = total_a + grecv_a[s].astype(F32)
-        total_b = total_b + grecv_b[s].astype(F32)
-    gout[me, 0 : 2 * share, :] = total_a.astype(BF16)
-    gout[me, 2 * share : 3 * share, :] = total_b.astype(BF16)
-
-    def send_out(peer):
-        remote(gout.at[me], gout.at[me], 14, peer, my).start()
-
-    peers(send_out)
-    lax.fori_loop(steps // 4, steps // 2, predict, 0)
-    wait_space(gout, 14)
-    whole = gout[...].astype(F32)
+    gather_sum(grecv_a, gout_a)
+    peers(send_out_a)
+    lax.fori_loop(quarter, steps // 2, predict, 0)
+    wait_space(gout_b, 15)
+    ge_ref[...] = gout_b[...].astype(F32).reshape(ge_ref.shape)
+    wait_space(gout_a, 14)
+    whole = gout_a[...].astype(F32)
     gd_ref[...] = whole[:, 0:share, :].reshape(gd_ref.shape)
     gp_ref[...] = whole[:, share : 2 * share, :].reshape(gp_ref.shape)
-    ge_ref[...] = whole[:, 2 * share : 3 * share, :].reshape(ge_ref.shape)
 
     sent(sendbuf, ns - 1, 0)
     sent(back, ns - 1, 1)
     sent(second_part, nc - 1, 2)
     sent(state_full, nc - 1, 3)
-    sent(first_full, nc - 1, 4)
+    sent(first_rows, nc - 1, 4)
+    sent(we_all, nc - 1, 16)
+    sent(wp_all, nc - 1, 17)
+    sent(state_rows, nc - 1, 18)
+    remote(seven, seven, 19, me, my).wait_send()
     sent(mid_full, nc - 1, 7)
     sent(out_rows, ns - 1, 10)
     sent(proj_part, nc - 1, 11)
     sent(grads_a, ns - 1, 12)
     sent(grads_b, ns - 1, 13)
-    sent(gout, ns - 1, 14)
+    sent(gout_a, ns - 1, 14)
+    sent(gout_b, ns - 1, 15)
 
 
 def local(
@@ -516,19 +610,24 @@
 
     vmem = pl.BlockSpec(memory_space=pltpu.VMEM)
     smem = pl.BlockSpec(memory_space=pltpu.SMEM)
-    weight = jax.ShapeDtypeStruct((full, width), F32)
+    weight = pltpu.VMEM((full, width), F32)
     return tuple(
         pl.pallas_call(
             functools.partial(kernel, (ns, nc, fan, fan_m, fan_d)),
             out_shape=(
-                jax.ShapeDtypeStruct(grid_state.shape, BF16),
+                pltpu.VMEM(grid_state.shape, BF16),
                 weight,
                 weight,
                 weight,
             ),
-            in_specs=[vmem] * 5 + [smem] + [vmem] * 4,
+            in_specs=[pl.BlockSpec(memory_space=pltpu.HBM)] * 5 + [smem] + [vmem] * 4,
             out_specs=(vmem,) * 4,
             scratch_shapes=[
+                pltpu.VMEM((grid_rows, width), BF16),
+                pltpu.VMEM((grid_rows, width), BF16),
+                pltpu.VMEM((nc, full, width), BF16),
+                pltpu.VMEM((nc, full, width), BF16),
+                pltpu.VMEM((full, width), BF16),
                 pltpu.VMEM((grid_rows, width), F32),
                 pltpu.VMEM((cap, width), F32),
                 pltpu.VMEM((ns, cap, width), BF16),
@@ -553,9 +652,10 @@
                 pltpu.VMEM((mesh, width), F32),
                 pltpu.VMEM((mesh, width), F32),
                 pltpu.VMEM((nc, mesh, width), BF16),
+                pltpu.VMEM((nc, mesh // nc, width), BF16),
                 pltpu.VMEM((mesh, width), F32),
-                pltpu.VMEM((mesh, width), F32),
-                pltpu.VMEM((nc, mesh, width), BF16),
+                pltpu.VMEM((nc, mesh // nc, full), BF16),
+                pltpu.VMEM((nc, mesh // nc, width), BF16),
                 pltpu.VMEM((mesh + 2 * reach, width), BF16),
                 pltpu.VMEM((nc, mesh, width), BF16),
                 pltpu.VMEM((ns, pad2, width), BF16),
@@ -570,10 +670,12 @@
                 pltpu.VMEM((ns, share, width), BF16),
                 pltpu.VMEM((ns, 2 * share, width), BF16),
                 pltpu.VMEM((ns, share, width), BF16),
-                pltpu.VMEM((ns, 3 * share, width), BF16),
-                pltpu.SemaphoreType.DMA((15,)),
-                pltpu.SemaphoreType.DMA((15,)),
+                pltpu.VMEM((ns, 2 * share, width), BF16),
+                pltpu.VMEM((ns, share, width), BF16),
+                pltpu.SemaphoreType.DMA((20,)),
+                pltpu.SemaphoreType.DMA((20,)),
                 pltpu.SemaphoreType.DMA((ns,)),
+                pltpu.SemaphoreType.DMA((5,)),
             ],
             compiler_params=pltpu.CompilerParams(
                 collective_id=0,

time: 100 us -> 91.7 us (0.917)
  Pallas kernels: 94.4 us -> 87.5 us
  local copies, waits for them, and re-layouts: 5.23 us -> 3.43 us
    pallas_call x1, Pallas kernels: 94.4 us -> 87.5 us  [local(): pl.pallas_call(functools.partial(kernel, (ns, nc, fan, fan_m, fan_d)), ou...]
    unnamed x10 -> x4, local copies, waits for them, and re-layouts: 5.23 us -> 3.43 us
where the time goes in v4:
time: 91.7 us; the launch traced here: 91.6 us
  Pallas kernels  87.5 us (95%)
  local copies, waits for them, and re-layouts  3.43 us (4%)
    pallas_call x1, Pallas kernels, local(): pl.pallas_call(functools.partial(kernel, (ns, nc, fan, fan_m, fan_d)), ou...  87.5 us
    unnamed x4, local copies, waits for them, and re-layouts  3.43 us

profile of v4, /device:TPU:1, one launch (start us, length us, event | category | flops | bytes accessed | tf_op | source)
XLA Modules:
  0.0 91.6 jit_solution(3429153804148778015)
XLA Ops:
  0.6 87.5 %encode_process_decode.1 = (bf16[8192,128]{1,0:T(8,128)(2,1)S(1)}, f32[512,128]{1,0:T(8,128)S(1)}, f32[512,128]{1,0:T(8,128)S(1)}, f32[512,128]{1,0:T(8,128)S(1)}) custom-call(bf16[8192,128]{1,0:T(8,128)(2,1)} %grid_hbm.1, bf16[8192,128]{1,0:T(8,128)(2,1)} %cot_hbm.1, bf16[512,128]{1,0:T(8,128)(2,1)} %we_hbm.1, bf16[512,128]{1,0:T(8,128)(2,1)} %wp_hbm.1, ...), custom_call_target="tpu_custom_call" | custom-call | flops 12000000000 | bytes 10000000 | tf_op jit(solution)/shard_map/encode_process_decode/pallas_call | solution.py:615
  88.1 1.3 %copy.18 = bf16[8192,128]{1,0:T(8,128)(2,1)} copy(bf16[8192,128]{1,0:T(8,128)(2,1)S(1)} %get-tuple-element.4) | data formatting | bytes 4194304
  89.4 0.7 copy.19
  90.2 0.7 copy.20
  90.9 0.7 copy.21

commit v5 on v4

--- a/solution.py
+++ b/solution.py
@@ -104,6 +104,10 @@
     proj_recv,
     grads_a,
     grads_b,
+    pair_a,
+    pair_b,
+    half_a,
+    half_b,
     grecv_a,
     grecv_b,
     gout_a,
@@ -122,7 +126,8 @@
     cap2 = mesh_send_ref.shape[1]
     pad2 = back.shape[1]
     reach = halo_low.shape[0]
-    share = grads_b.shape[1]
+    share = grads_b.shape[2]
+    full = ge_ref.shape[0]
     fan_scale = fan ** (-0.5)
     fan_m_scale = fan_m ** (-0.5)
     fan_d_scale = fan_d ** (-0.5)
@@ -492,36 +497,59 @@
 
     peers(send_rows)
     slots[me] = out_rows[me]
-    blocks = width // share
-
-    def split(grad):
-        return grad.astype(BF16).reshape(blocks, share, width)
+    core = lax.rem(me, 2)
+    pair = me // 2
+    sibling = me + 1 - 2 * core
+    pairs = ns // 2
+    blocks = width // share // 2
+
+    def deal(buf, c, rows, grad):
+        parts = grad.reshape(blocks, 2, share, width)
+        for u in range(2):
+            buf[u, c * blocks : (c + 1) * blocks, rows, :] = parts[:, u]
+
+    def same_core(body):
+        def step(k, carry):
+            body(lax.rem(me + 2 * k, ns) if side == 1 else at_distance(k, 1))
+            return carry
+
+        lax.fori_loop(1, pairs, step, 0)
+
+    def wait_pairs(buf, which):
+        part = buf.at[pl.ds(0, pairs - 1)]
+        remote(part, part, which, me, my).wait_recv()
 
     for c in range(nc):
-        cut = slice(c * blocks, (c + 1) * blocks)
-        grads_a[cut, 0:share, :] = split(dot_tn(mid_full[c], dgrad[...]))
-        grads_a[cut, share : 2 * share, :] = split(
-            dot_tn(first_rows[:, :, c * width : (c + 1) * width].reshape(mesh, width), projected)
-        )
-
-    def send_a(peer):
-        remote(grads_a.at[peer], grecv_a.at[me], 12, peer, my).start()
-
-    peers(send_a)
-    grecv_a[me] = grads_a[me]
+        deal(grads_a, c, slice(0, share), dot_tn(mid_full[c], dgrad[...]))
+        latent = first_rows[:, :, c * width : (c + 1) * width].reshape(mesh, width)
+        deal(grads_a, c, slice(share, 2 * share), dot_tn(latent, projected))
+
+    swap_a = remote(grads_a.at[1 - core], pair_a, 12, sibling, my)
+    swap_a.start()
     wait_chan(proj_recv, 11)
     total = second[...]
     for c in range(nc):
         total = total + proj_recv[c].astype(F32)
     sum_grad = (total * gathered[...]).astype(BF16)
     for c in range(nc):
-        grads_b[c * blocks : (c + 1) * blocks] = split(dot_tn(state_full[c], sum_grad))
+        deal(grads_b, c, slice(0, share), dot_tn(state_full[c], sum_grad))
+    swap_b = remote(grads_b.at[1 - core], pair_b, 13, sibling, my)
+    swap_b.start()
+    swap_a.wait()
+    half_a[...] = (grads_a[core] + pair_a[...]).astype(BF16)
+    grecv_a[pair] = half_a[pair]
+
+    def send_a(peer):
+        remote(half_a.at[peer // 2], grecv_a.at[pair], 20, peer, my).start()
 
     def send_b(peer):
-        remote(grads_b.at[peer], grecv_b.at[me], 13, peer, my).start()
-
-    peers(send_b)
-    grecv_b[me] = grads_b[me]
+        remote(half_b.at[peer // 2], grecv_b.at[pair], 21, peer, my).start()
+
+    swap_b.wait()
+    half_b[...] = (grads_b[core] + pair_b[...]).astype(BF16)
+    grecv_b[pair] = half_b[pair]
+    same_core(send_b)
+    same_core(send_a)
 
     wait_space(slots, 10)
     rows = slots[...].astype(F32)[:, 0:cap2, :].reshape(all_slots, width)
@@ -536,31 +564,45 @@
 
     def gather_sum(got, whole):
         total = got[0].astype(F32)
-        for source in range(1, ns):
+        for source in range(1, pairs):
             total = total + got[source].astype(F32)
-        whole[me] = total.astype(BF16)
+        whole[core, pair] = total.astype(BF16)
 
     def send_out_a(peer):
-        remote(gout_a.at[me], gout_a.at[me], 14, peer, my).start()
+        mine = gout_a.at[core, pair]
+        remote(mine, mine, 14, peer, my).start()
 
     def send_out_b(peer):
-        remote(gout_b.at[me], gout_b.at[me], 15, peer, my).start()
-
-    quarter = max(steps // 8, 1)
-    lax.fori_loop(0, quarter, predict, 0)
-    wait_space(grecv_b, 13)
+        mine = gout_b.at[core, pair]
+        remote(mine, mine, 15, peer, my).start()
+
+    cuts = [i * (steps // 2) // 4 for i in range(5)]
+    lax.fori_loop(cuts[0], cuts[1], predict, 0)
+    wait_pairs(grecv_b, 21)
     gather_sum(grecv_b, gout_b)
-    peers(send_out_b)
-    wait_space(grecv_a, 12)
+    same_core(send_out_b)
+    wait_pairs(grecv_a, 20)
     gather_sum(grecv_a, gout_a)
-    peers(send_out_a)
-    lax.fori_loop(quarter, steps // 2, predict, 0)
-    wait_space(gout_b, 15)
-    ge_ref[...] = gout_b[...].astype(F32).reshape(ge_ref.shape)
-    wait_space(gout_a, 14)
-    whole = gout_a[...].astype(F32)
-    gd_ref[...] = whole[:, 0:share, :].reshape(gd_ref.shape)
-    gp_ref[...] = whole[:, share : 2 * share, :].reshape(gp_ref.shape)
+    same_core(send_out_a)
+    lax.fori_loop(cuts[1], cuts[2], predict, 0)
+    wait_pairs(gout_b.at[core], 15)
+    twin_b = remote(gout_b.at[core], gout_b.at[core], 23, sibling, my)
+    twin_b.start()
+    lax.fori_loop(cuts[2], cuts[3], predict, 0)
+    wait_pairs(gout_a.at[core], 14)
+    twin_a = remote(gout_a.at[core], gout_a.at[core], 22, sibling, my)
+    twin_a.start()
+    lax.fori_loop(cuts[3], cuts[4], predict, 0)
+
+    def joined(buf, rows):
+        both = jnp.stack([buf[0, :, rows, :], buf[1, :, rows, :]], axis=1)
+        return both.astype(F32).reshape(full, width)
+
+    twin_b.wait()
+    ge_ref[...] = joined(gout_b, slice(0, share))
+    twin_a.wait()
+    gd_ref[...] = joined(gout_a, slice(0, share))
+    gp_ref[...] = joined(gout_a, slice(share, 2 * share))
 
     sent(sendbuf, ns - 1, 0)
     sent(back, ns - 1, 1)
@@ -574,10 +616,10 @@
     sent(mid_full, nc - 1, 7)
     sent(out_rows, ns - 1, 10)
     sent(proj_part, nc - 1, 11)
-    sent(grads_a, ns - 1, 12)
-    sent(grads_b, ns - 1, 13)
-    sent(gout_a, ns - 1, 14)
-    sent(gout_b, ns - 1, 15)
+    sent(half_a, pairs - 1, 20)
+    sent(half_b, pairs - 1, 21)
+    sent(half_a, pairs - 1, 14)
+    sent(half_b, pairs - 1, 15)
 
 
 def local(
@@ -666,14 +708,18 @@
                 pltpu.VMEM((reach, width), F32),
                 pltpu.VMEM((nc, mesh, width), BF16),
                 pltpu.VMEM((nc, mesh, width), BF16),
-                pltpu.VMEM((ns, 2 * share, width), BF16),
-                pltpu.VMEM((ns, share, width), BF16),
-                pltpu.VMEM((ns, 2 * share, width), BF16),
-                pltpu.VMEM((ns, share, width), BF16),
-                pltpu.VMEM((ns, 2 * share, width), BF16),
-                pltpu.VMEM((ns, share, width), BF16),
-                pltpu.SemaphoreType.DMA((20,)),
-                pltpu.SemaphoreType.DMA((20,)),
+                pltpu.VMEM((2, ns // 2, 2 * share, width), F32),
+                pltpu.VMEM((2, ns // 2, share, width), F32),
+                pltpu.VMEM((ns // 2, 2 * share, width), F32),
+                pltpu.VMEM((ns // 2, share, width), F32),
+                pltpu.VMEM((ns // 2, 2 * share, width), BF16),
+                pltpu.VMEM((ns // 2, share, width), BF16),
+                pltpu.VMEM((ns // 2, 2 * share, width), BF16),
+                pltpu.VMEM((ns // 2, share, width), BF16),
+                pltpu.VMEM((2, ns // 2, 2 * share, width), BF16),
+                pltpu.VMEM((2, ns // 2, share, width), BF16),
+                pltpu.SemaphoreType.DMA((24,)),
+                pltpu.SemaphoreType.DMA((24,)),
                 pltpu.SemaphoreType.DMA((ns,)),
                 pltpu.SemaphoreType.DMA((5,)),
             ],

time: 91.7 us -> 89 us (0.971)
  Pallas kernels: 87.5 us -> 84.8 us
    pallas_call x1, Pallas kernels: 87.5 us -> 84.8 us  [local(): pl.pallas_call(functools.partial(kernel, (ns, nc, fan, fan_m, fan_d)), ou...]
where the time goes in v5:
time: 89 us; the launch traced here: 88.8 us
  Pallas kernels  84.8 us (95%)
  local copies, waits for them, and re-layouts  3.43 us (4%)
    pallas_call x1, Pallas kernels, local(): pl.pallas_call(functools.partial(kernel, (ns, nc, fan, fan_m, fan_d)), ou...  84.8 us
    unnamed x4, local copies, waits for them, and re-layouts  3.43 us

profile of v5, /device:TPU:1, one launch (start us, length us, event | category | flops | bytes accessed | tf_op | source)
XLA Modules:
  0.0 88.8 jit_solution(18424698682931833844)
XLA Ops:
  0.6 84.8 %encode_process_decode.1 = (bf16[8192,128]{1,0:T(8,128)(2,1)S(1)}, f32[512,128]{1,0:T(8,128)S(1)}, f32[512,128]{1,0:T(8,128)S(1)}, f32[512,128]{1,0:T(8,128)S(1)}) custom-call(bf16[8192,128]{1,0:T(8,128)(2,1)} %grid_hbm.1, bf16[8192,128]{1,0:T(8,128)(2,1)} %cot_hbm.1, bf16[512,128]{1,0:T(8,128)(2,1)} %we_hbm.1, bf16[512,128]{1,0:T(8,128)(2,1)} %wp_hbm.1, ...), custom_call_target="tpu_custom_call" | custom-call | flops 12000000000 | bytes 10000000 | tf_op jit(solution)/shard_map/encode_process_decode/pallas_call | solution.py:657
  85.4 1.3 %copy.18 = bf16[8192,128]{1,0:T(8,128)(2,1)} copy(bf16[8192,128]{1,0:T(8,128)(2,1)S(1)} %get-tuple-element.4) | data formatting | bytes 4194304
  86.7 0.7 copy.19
  87.4 0.7 copy.20
  88.1 0.7 copy.21
